TPU v7x, 32 devices: a whole 2x2x4 slice. The times are simulated.
32 devices in a mesh: img: 8 (over z, y), head: 4 (over x, core).
Axes of the slice: x: 2, y: 2, z: 4, core: 2. Of those that a mesh axis runs over, the one named last changes fastest.
Arguments:
- tokens: bfloat16 [192, 197, 768], P(('img', 'head')), may hold values from -6 to 6
- slot_ids: int32 [192, 160], P(('img', 'head')), may hold values from 0 to 196, as said below
- counts: int32 [192], P(('img', 'head')), may hold values from 39 to 157
- w_qkv: bfloat16 [768, 2304], P(None, 'head'), may hold values from -0.21875 to 0.21875
- w_out: bfloat16 [768, 768], P('head'), may hold values from -0.875 to 0.875
- w_up: bfloat16 [768, 3072], replicated, may hold values from -0.21875 to 0.21875
- w_down: bfloat16 [3072, 768], replicated, may hold values from -0.109375 to 0.109375
- gain_one: float32 [768], replicated, may hold values from 0.5 to 1.5
- bias_one: float32 [768], replicated, may hold values from -2 to 2
- gain_two: float32 [768], replicated, may hold values from 0.5 to 1.5
- bias_two: float32 [768], replicated, may hold values from -2 to 2
- w_router: float32 [768], replicated, may hold values from -0.21875 to 0.21875
- cotangent: bfloat16 [192, 197, 768], P(('img', 'head')), may hold values from -6 to 6
Outputs:
- result: bfloat16 [192, 197, 768], P(('img', 'head'))
- grad_tokens: float32 [192, 197, 768], P(('img', 'head'))
- grad_qkv: float32 [768, 2304], P(None, 'head')
- grad_out: float32 [768, 768], P('head')
- grad_up: float32 [768, 3072], P(None, 'head')
- grad_down: float32 [3072, 768], P('head')
- grad_gain_one: float32 [768], P('head')
- grad_bias_one: float32 [768], P('head')
- grad_gain_two: float32 [768], P('head')
- grad_bias_two: float32 [768], P('head')
- grad_router: float32 [768], P('head')
Inputs may be any that keep to these rules, and one draw needn't show every extreme that they name: `slot_ids`: within each image the 160 slots hold distinct token numbers; the first counts of them are the routed tokens.
All inputs are finite; a program needn't handle non-finite values.
Results may differ from a plain program's by a relative error of at most 0.012.
The roundings to bfloat16 on the way count: a program that leaves them out, or rounds other values in their place, can miss the bound.
Values may be sent and summed in bfloat16 or wider, within the bound.
A program may use at most 256 MiB of HBM per device.

v0:
```python
import jax
import jax.numpy as jnp
from jax import lax
from jax.sharding import PartitionSpec as P

HEAD_DIM = 64


def layer_norm(values, norm_gain, norm_bias):
    average = jnp.mean(values, axis=-1, keepdims=True)
    centred = values - average
    variance = jnp.mean(centred * centred, axis=-1, keepdims=True)
    return centred * lax.rsqrt(variance + 1e-06) * norm_gain + norm_bias


def gelu_exact(values):
    return jax.nn.gelu(values, approximate=False)


def select_rows(matrix, indices):
    return jax.vmap(lambda image_rows, positions: image_rows[positions])(matrix, indices)


def add_rows(matrix, indices, additions):
    return jax.vmap(lambda image_rows, positions, addend: image_rows.at[positions].add(addend))(
        matrix, indices, additions
    )


def masked_scores(query_rows, key_rows, key_valid):
    score_scale = query_rows.shape[-1] ** (-0.5)
    scores = (
        jnp.einsum("gqhe,gkhe->ghqk", query_rows, key_rows, preferred_element_type=jnp.float32)
        * score_scale
    )
    return jnp.where(key_valid[:, None, None, :], scores, -1e30)


def attend_forward(normed, key_valid, w_qkv):
    images, capacity, features = normed.shape
    projected = jnp.dot(
        normed.reshape(images * capacity, features), w_qkv, preferred_element_type=jnp.float32
    ).astype(jnp.bfloat16)
    projected = projected.reshape(images, capacity, -1, 3, HEAD_DIM)
    query_rows = projected[:, :, :, 0]
    key_rows = projected[:, :, :, 1]
    value_rows = projected[:, :, :, 2]
    scores = masked_scores(query_rows, key_rows, key_valid)
    highest = jnp.max(scores, axis=-1, keepdims=True)
    expo_terms = jnp.exp(scores - highest)
    totals = jnp.sum(expo_terms, axis=-1, keepdims=True)
    weights_b = (expo_terms / totals).astype(jnp.bfloat16)
    mixed_heads = jnp.einsum(
        "ghqk,gkhe->gqhe", weights_b, value_rows, preferred_element_type=jnp.float32
    ).astype(jnp.bfloat16)
    log_totals = highest + jnp.log(totals)
    return (
        mixed_heads.reshape(images * capacity, -1),
        (query_rows, key_rows, value_rows, log_totals),
    )


def attend_backward(normed, key_valid, kept_state, grad_mixed):
    query_rows, key_rows, value_rows, log_totals = kept_state
    images, capacity, head_count, head_size = query_rows.shape
    score_scale = head_size ** (-0.5)
    probs_full = jnp.exp(masked_scores(query_rows, key_rows, key_valid) - log_totals)
    grad_heads = grad_mixed.reshape(images, capacity, head_count, head_size)
    grad_value = jnp.einsum(
        "ghqk,gqhe->gkhe",
        probs_full.astype(jnp.bfloat16),
        grad_heads,
        preferred_element_type=jnp.float32,
    )
    grad_probs = jnp.einsum(
        "gqhe,gkhe->ghqk", grad_heads, value_rows, preferred_element_type=jnp.float32
    )
    grad_scores = probs_full * (
        grad_probs - jnp.sum(probs_full * grad_probs, axis=-1, keepdims=True)
    )
    grad_scores = grad_scores.astype(jnp.bfloat16)
    grad_query = (
        jnp.einsum("ghqk,gkhe->gqhe", grad_scores, key_rows, preferred_element_type=jnp.float32)
        * score_scale
    )
    grad_key = (
        jnp.einsum("ghqk,gqhe->gkhe", grad_scores, query_rows, preferred_element_type=jnp.float32)
        * score_scale
    )
    grad_proj = (
        jnp.stack([grad_query, grad_key, grad_value], axis=3)
        .astype(jnp.bfloat16)
        .reshape(images * capacity, -1)
    )
    grad_wqkv_t = jnp.einsum(
        "rc,rd->cd",
        grad_proj,
        normed.reshape(images * capacity, -1),
        preferred_element_type=jnp.float32,
    )
    return (grad_proj, grad_wqkv_t)


def shards(
    tokens,
    slot_ids,
    counts,
    w_qkv,
    w_out,
    w_up,
    w_down,
    gain_one,
    bias_one,
    gain_two,
    bias_two,
    w_router,
    cotangent,
):
    owned, length, features = tokens.shape
    capacity = slot_ids.shape[1]
    own_rows = owned * capacity
    picked = select_rows(tokens, slot_ids).astype(jnp.float32)
    own_valid = jnp.arange(capacity)[None, :] < counts[:, None]
    slot_mask = own_valid.astype(jnp.float32)
    normed_f, norm_pull = jax.vjp(layer_norm, picked, gain_one, bias_one)
    normed_one = normed_f.astype(jnp.bfloat16)
    group_normed, group_counts = (
        lax.all_gather(normed_one, "head", axis=0, tiled=True),
        lax.all_gather(counts, "head", axis=0, tiled=True),
    )
    group_valid = jnp.arange(capacity)[None, :] < group_counts[:, None]
    mixed_heads, kept_state = attend_forward(group_normed, group_valid, w_qkv)
    attn_out = lax.psum_scatter(
        jnp.dot(mixed_heads, w_out, preferred_element_type=jnp.float32),
        "head",
        scatter_dimension=0,
        tiled=True,
    ).reshape(owned, capacity, features)
    hidden_in = picked + attn_out
    normed_two_f, norm_two_pull = jax.vjp(layer_norm, hidden_in, gain_two, bias_two)
    normed_two = normed_two_f.astype(jnp.bfloat16).reshape(own_rows, features)
    pre_act = jnp.dot(normed_two, w_up, preferred_element_type=jnp.float32)
    activated, act_pull = jax.vjp(gelu_exact, pre_act)
    activated_b = activated.astype(jnp.bfloat16)
    mlp_out = jnp.dot(activated_b, w_down, preferred_element_type=jnp.float32).reshape(
        owned, capacity, features
    )
    gate_value = jax.nn.sigmoid(jnp.sum(picked * w_router, axis=-1))
    weight_row = gate_value * slot_mask
    branch = attn_out + mlp_out
    result = add_rows(tokens.astype(jnp.float32), slot_ids, weight_row[..., None] * branch).astype(
        jnp.bfloat16
    )
    grad_picked_out = select_rows(cotangent, slot_ids).astype(jnp.float32)
    grad_branch = weight_row[..., None] * grad_picked_out
    grad_gate = slot_mask * jnp.sum(grad_picked_out * branch, axis=-1)
    grad_logits = grad_gate * gate_value * (1.0 - gate_value)
    grad_router = jnp.einsum("ic,icd->d", grad_logits, picked)
    grad_mlp = grad_branch.astype(jnp.bfloat16).reshape(own_rows, features)
    grad_down = jnp.einsum("rf,rd->fd", activated_b, grad_mlp, preferred_element_type=jnp.float32)
    grad_act = jnp.einsum("rd,fd->rf", grad_mlp, w_down, preferred_element_type=jnp.float32)
    grad_pre = act_pull(grad_act)[0].astype(jnp.bfloat16)
    grad_up_t = jnp.einsum("rf,rd->fd", grad_pre, normed_two, preferred_element_type=jnp.float32)
    grad_normed_two = jnp.einsum(
        "rf,df->rd", grad_pre, w_up, preferred_element_type=jnp.float32
    ).reshape(owned, capacity, features)
    grad_hidden, grad_gain_two, grad_bias_two = norm_two_pull(grad_normed_two)
    grad_attn_b = (grad_branch + grad_hidden).astype(jnp.bfloat16).reshape(own_rows, features)
    group_grad = lax.all_gather(grad_attn_b, "head", axis=0, tiled=True)
    grad_mixed = jnp.einsum(
        "rd,ed->re", group_grad, w_out, preferred_element_type=jnp.float32
    ).astype(jnp.bfloat16)
    grad_wout = jnp.einsum("re,rd->ed", mixed_heads, group_grad, preferred_element_type=jnp.float32)
    grad_proj, grad_wqkv_t = attend_backward(group_normed, group_valid, kept_state, grad_mixed)
    grad_normed = lax.psum_scatter(
        jnp.einsum("rc,dc->rd", grad_proj, w_qkv, preferred_element_type=jnp.float32),
        "head",
        scatter_dimension=0,
        tiled=True,
    ).reshape(owned, capacity, features)
    grad_picked, grad_gain_one, grad_bias_one = norm_pull(grad_normed)
    grad_rows = grad_picked + grad_hidden + grad_logits[..., None] * w_router
    grad_tokens = add_rows(cotangent.astype(jnp.float32), slot_ids, grad_rows)
    up_part, down_part, gain_one_part, bias_one_part, gain_two_part, bias_two_part, router_part = (
        lax.psum_scatter(grad_up_t, "head", scatter_dimension=0, tiled=True),
        lax.psum_scatter(grad_down, "head", scatter_dimension=0, tiled=True),
        lax.psum_scatter(grad_gain_one, "head", scatter_dimension=0, tiled=True),
        lax.psum_scatter(grad_bias_one, "head", scatter_dimension=0, tiled=True),
        lax.psum_scatter(grad_gain_two, "head", scatter_dimension=0, tiled=True),
        lax.psum_scatter(grad_bias_two, "head", scatter_dimension=0, tiled=True),
        lax.psum_scatter(grad_router, "head", scatter_dimension=0, tiled=True),
    )
    qkv_part, out_part = (grad_wqkv_t, grad_wout)
    summed = lax.psum(
        (
            qkv_part,
            out_part,
            up_part,
            down_part,
            gain_one_part,
            bias_one_part,
            gain_two_part,
            bias_two_part,
            router_part,
        ),
        "img",
    )
    return (
        result,
        grad_tokens,
        summed[0].T,
        summed[1],
        summed[2].T,
        summed[3],
        summed[4],
        summed[5],
        summed[6],
        summed[7],
        summed[8],
    )


def solution(mesh):
    return jax.shard_map(
        shards,
        mesh=mesh,
        in_specs=(
            P(("img", "head"), None, None),
            P(("img", "head"), None),
            P(("img", "head")),
            P(None, "head"),
            P("head", None),
            P(),
            P(),
            P(),
            P(),
            P(),
            P(),
            P(),
            P(("img", "head"), None, None),
        ),
        out_specs=(
            P(("img", "head"), None, None),
            P(("img", "head"), None, None),
            P(None, "head"),
            P("head", None),
            P(None, "head"),
            P("head", None),
            P("head"),
            P("head"),
            P("head"),
            P("head"),
            P("head"),
        ),
        check_vma=False,
    )
```

profile of v0, /device:TPU:0, one launch (start us, length us, event | category | flops | bytes accessed | tf_op | source)
XLA Modules:
  0.0 1173.9 jit_solution(7991414762496175141)
XLA Ops:
  7.2 1.4 fusion.36
  8.7 14.3 %gather_fusion = bf16[960,768]{1,0:T(8,128)(2,1)S(1)} fusion(bf16[6,197,768]{2,1,0:T(8,128)(2,1)} %param.13, s32[960]{0:T(1024)S(1)} %reshape.320), kind=kCustom, calls=%fused_computation | custom fusion | bytes 2956800 | tf_op jit(solution)/shard_map/vmap()/gather | solution.py:21
  23.1 0.6 multiply_reduce_fusion.7
  23.7 0.6 multiply_reduce_fusion.6
  25.0 1.7 add_convert_fusion.2
  28.3 6.5 all-reduce
  34.9 38.8 %all-gather.3.cloned.1.call-done = bf16[24,160,768]{2,1,0:T(8,128)(2,1)} async-done(((bf16[6,160,768]{2,1,0:T(8,128)(2,1)}), bf16[24,160,768]{2,1,0:T(8,128)(2,1)}) %all-gather.3.cloned.1.call-update) | async-done | bytes 5898256 | tf_op jit(solution)/shard_map/all_gather | solution.py:128
  73.7 7.9 convolution_convert_fusion
  81.6 12.7 %reshape.309 = bf16[24,160,3,3,64]{1,0,4,3,2:T(8,128)(2,1)} reshape(bf16[3840,576]{0,1:T(8,128)(2,1)} %convolution_convert_fusion) | data formatting | bytes 8847360 | tf_op jit(solution)/shard_map/reshape | solution.py:44
  94.3 3.6 fusion.53
  97.9 3.8 fusion.12
  101.8 3.5 fusion.6
  105.3 0.8 copy-done.3
  106.3 4.6 convert_bitcast_fusion
  110.9 2.8 copy.50
  113.6 4.9 reshape.310
  118.5 7.5 fusion.56
  126.6 17.5 %gather_fusion.1 = bf16[960,768]{1,0:T(8,128)(2,1)} fusion(bf16[6,197,768]{2,1,0:T(8,128)(2,1)} %param.25, s32[960]{0:T(1024)S(1)} %reshape.320), kind=kCustom, calls=%fused_computation.1 | custom fusion | bytes 2956800 | tf_op jit(solution)/shard_map/vmap()/gather | solution.py:21
  144.1 75.9 %reduce-scatter.5.cloned.1.call-done = f32[960,768]{1,0:T(8,128)} async-done(((f32[3840,768]{1,0:T(8,128)}), f32[960,768]{1,0:T(8,128)}) %reduce-scatter.5.cloned.1.call-update) | async-done | bytes 2949136 | tf_op jit(solution)/shard_map/reduce_scatter | solution.py:133
  220.0 2.2 fusion.52
  222.8 1.0 multiply_add_fusion.1
  223.8 33.7 %multiply_convert_fusion.1 = (bf16[960,3072]{1,0:T(8,128)(2,1)}, f32[960,3072]{1,0:T(8,128)}, f32[960,3072]{1,0:T(8,128)}) fusion(bf16[768,3072]{1,0:T(8,128)(2,1)} %param.18, f32[960,768]{1,0:T(8,128)S(1)} %get-tuple-element.73, f32[768]{0:T(1024)S(1)} %copy-done.48, f32[768]{0:T(1024)S(1)} %copy-done.43, f32[960]{0:T(1024)S(1)} %get-tuple-element.90, ...), kind=kOutput, calls=%fused_computation.11 | convolution fusion | flops 4725227520 | bytes 37172736 | tf_op jit(solution)/shard_map/dot_general | solution.py:142
  257.5 17.2 %add_convert_fusion = bf16[960,3072]{1,0:T(8,128)(2,1)} fusion(f32[960,3072]{1,0:T(8,128)} %get-tuple-element.71, f32[960,3072]{1,0:T(8,128)} %get-tuple-element.95, bf16[3072,768]{1,0:T(8,128)(2,1)} %param.19, bf16[960,768]{1,0:T(8,128)(2,1)} %gather_fusion.1, f32[960]{0:T(1024)S(1)} %reshape.318), kind=kOutput, calls=%fused_computation.9 | convolution fusion | flops 4573347840 | bytes 35688192 | tf_op jit(solution)/shard_map/rd,fd->rf/dot_general | solution.py:161
  274.7 9.5 multiply_reduce_fusion.1
  284.3 1.1 fusion.50
  285.9 1.3 copy-done.9
  287.6 9.5 fusion.16
  297.1 11.0 fusion.48
  308.2 1.3 copy-done.17
  309.5 10.6 fusion.29
  320.2 0.8 copy-done.20
  321.1 20.3 %all-gather.5.cloned.1.call-done = bf16[3840,768]{1,0:T(8,128)(2,1)} async-done(((bf16[960,768]{1,0:T(8,128)(2,1)}), bf16[3840,768]{1,0:T(8,128)(2,1)}) %all-gather.5.cloned.1.call-update) | async-done | bytes 5898256 | tf_op jit(solution)/shard_map/all_gather | solution.py:169
  341.4 4.7 convolution_convert_fusion.1
  346.1 4.4 reshape.313
  350.6 14.6 %multiply_reduce_fusion = (f32[24,3,160]{2,1,0:T(4,128)S(1)}, f32[24,3,160,160]{2,3,1,0:T(8,128)S(1)}) fusion(f32[24,3,160]{2,1,0:T(4,128)S(1)} %log_add_fusion, f32[24,3,160,160]{2,3,1,0:T(8,128)} %copy-done.3, pred[24,160]{1,0:T(8,128)(4,1)S(1)} %copy-done.28, bf16[24,160,3,1,64]{1,0,4,3,2:T(8,128)(2,1)} %copy-done.12, bf16[24,160,3,64]{1,0,3,2:T(8,128)(2,1)} %reshape.313), kind=kOutput, calls=%fused_computation.8 | convolution fusion | flops 245134080 | bytes 17790720 | tf_op jit(solution)/shard_map/gqhe,gkhe->ghqk/dot_general | solution.py:75
  365.2 6.8 multiply_convert_fusion
  372.1 5.2 multiply_bitcast_fusion
  377.3 4.5 multiply_bitcast_fusion.1
  381.8 6.4 fusion.22
  388.1 4.6 maximum_convert_fusion
  392.8 7.3 copy.56
  400.1 12.1 %convert_element_type.115 = bf16[3840,576]{0,1:T(8,128)(2,1)} reshape(bf16[24,160,3,3,64]{1,0,4,3,2:T(8,128)(2,1)} %copy.56) | data formatting | bytes 8847360 | tf_op jit(solution)/shard_map/convert_element_type | solution.py:92
  412.1 5.0 fusion.58
  417.1 7.5 fusion.59
  424.6 78.6 %reduce-scatter.11.cloned.1.call-done = f32[768,768]{1,0:T(8,128)} async-done(((f32[3072,768]{1,0:T(8,128)}), f32[768,768]{1,0:T(8,128)}) %reduce-scatter.11.cloned.1.call-update) | async-done | bytes 2359312 | tf_op jit(solution)/shard_map/reduce_scatter | solution.py:186
  503.3 10.0 fusion.57
  513.3 0.7 copy-done.26
  514.0 1.1 copy-done.4
  515.1 2.1 convert_element_type.105
  517.3 2.1 convert_element_type.93
  521.0 223.0 %all-reduce.11.cloned.1.call-done = (f32[768,576]{0,1:T(8,128)}, f32[192,768]{1,0:T(8,128)}, f32[768,768]{0,1:T(8,128)}, f32[768,768]{1,0:T(8,128)}) async-done(((f32[768,576]{0,1:T(8,128)}, f32[192,768]{1,0:T(8,128)}, f32[768,768]{0,1:T(8,128)}, f32[768,768]{1,0:T(8,128)}), (f32[768,576]{0,1:T(8,128)}, f32[192,768]{1,0:T(8,128)}, f32[768,768]{0,1:T(8,128)}, ...) | async-done | bytes 7077904 | tf_op jit(solution)/shard_map/psum | solution.py:194
  744.0 3.0 copy.57
  747.0 92.7 %reduce-scatter.7.cloned.1.call-done = f32[960,768]{1,0:T(8,128)} async-done(((f32[3840,768]{1,0:T(8,128)}), f32[960,768]{1,0:T(8,128)}) %reduce-scatter.7.cloned.1.call-update) | async-done | bytes 2949136 | tf_op jit(solution)/shard_map/reduce_scatter | solution.py:175
  839.7 4.1 multiply_reduce_fusion.3
  844.0 4.2 multiply_reduce_fusion.2
  848.3 10.3 all-reduce.8
  859.0 8.6 fusion.19
  867.6 134.2 %scatter_fusion = f32[6,197,768]{2,1,0:T(8,128)} fusion(f32[6,197,768]{2,1,0:T(8,128)} %convert_element_type.93, s32[960]{0:T(1024)S(1)} %reshape.332, f32[960,768]{1,0:T(8,128)} %bitcast.109), kind=kCustom, calls=%fused_computation.2 | custom fusion | flops 737280 | bytes 8855040 | tf_op jit(solution)/shard_map/vmap()/scatter-add | solution.py:25
  1001.9 3.5 convert_element_type.104
  1005.3 134.1 %scatter_fusion.1 = f32[6,197,768]{2,1,0:T(8,128)} fusion(f32[6,197,768]{2,1,0:T(8,128)} %convert_element_type.105, s32[960]{0:T(1024)S(1)} %reshape.332, f32[960,768]{1,0:T(8,128)} %bitcast.108), kind=kCustom, calls=%fused_computation.3 | custom fusion | flops 737280 | bytes 8855040 | tf_op jit(solution)/shard_map/vmap()/scatter-add | solution.py:25
  1139.4 22.3 %all-reduce.6 = (f32[192]{0:T(256)}, f32[192]{0:T(256)}, f32[192]{0:T(256)}, f32[192]{0:T(256)}, f32[192]{0:T(256)}) all-reduce(f32[192]{0:T(256)S(1)} %dynamic-slice.2, f32[192]{0:T(256)S(1)} %dynamic-slice.4, f32[192]{0:T(256)S(1)} %dynamic-slice.6, f32[192]{0:T(256)S(1)} %dynamic-slice.8, ...), channel_id=1, replica_groups=mesh['img'=8,'head'=4] {'img'}, use_global_device_ids=true, to_apply=%region_25.26 | all-reduce | flops 960 | bytes 7680 | tf_op jit(solution)/shard_map/psum | solution.py:194
  1161.7 2.9 copy.98
  1164.6 0.8 copy.99
  1165.4 1.4 copy.100
  (151 shorter events, 6.0 us)
Async XLA Ops:
  7.2 66.5 %copy-start = (bf16[768,576]{0,1:T(8,128)(2,1)S(1)}, bf16[768,576]{0,1:T(8,128)(2,1)}, u32[]{:S(2)}) copy-start(bf16[768,576]{0,1:T(8,128)(2,1)} %param.16) | copy-start | bytes 2654212
  7.2 66.5 %all-gather.3.cloned.1.call-start = ((), (), s32[]{:S(2)}) async-start(), calls=%async_computation.4 | async-start | bytes 7372800 | tf_op jit(solution)/shard_map/all_gather | solution.py:128
  8.7 14.4 %copy-start.41 = (f32[768]{0:T(1024)S(1)}, f32[768]{0:T(1024)}, u32[]{:S(2)}) copy-start(f32[768]{0:T(1024)} %param.24) | copy-start | bytes 9220
  23.0 197.0 %copy-start.1 = (bf16[960,768]{1,0:T(8,128)(2,1)}, bf16[960,768]{1,0:T(8,128)(2,1)S(1)}, u32[]{:S(2)}) copy-start(bf16[960,768]{1,0:T(8,128)(2,1)S(1)} %gather_fusion) | copy-start | bytes 4423684
  23.0 1.9 copy-start.37
  23.1 1.9 copy-start.44
  23.7 102.8 %copy-start.31 = (f32[6,160]{1,0:T(8,128)}, f32[6,160]{1,0:T(8,128)S(1)}, u32[]{:S(2)}) copy-start(f32[6,160]{1,0:T(8,128)S(1)} %get-tuple-element.50) | copy-start | bytes 11524
  23.7 0.7 copy-start.25
  23.7 3.0 copy-start.47
  23.7 4.3 copy-start.45
  24.3 3.9 copy-start.35
  24.4 0.6 copy-start.29
  26.7 193.3 %reduce-scatter.5.cloned.1.call-start = ((), (), s32[]{:S(2)}) async-start(), calls=%async_computation.5 | async-start | bytes 14745600 | tf_op jit(solution)/shard_map/reduce_scatter | solution.py:133
  34.9 70.4 %copy-start.27 = (pred[24,160]{1,0:T(8,128)(4,1)}, pred[24,160]{1,0:T(8,128)(4,1)S(1)}, u32[]{:S(2)}) copy-start(pred[24,160]{1,0:T(8,128)(4,1)S(1)} %iota_compare_fusion) | copy-start | bytes 11524
  97.8 3.9 copy-start.8
  97.9 3.9 copy-start.11
  97.9 7.4 copy-start.12
  101.7 4.4 copy-start.3
  101.7 4.5 copy-start.19
  105.3 5.6 copy-start.21
  113.6 4.9 copy-start.23
  126.0 215.4 %all-gather.5.cloned.1.call-start = ((), (), s32[]{:S(2)}) async-start(), calls=%async_computation.6 | async-start | bytes 7372800 | tf_op jit(solution)/shard_map/all_gather | solution.py:169
  126.5 17.6 %copy-start.33 = (f32[6,160]{1,0:T(8,128)}, f32[6,160]{1,0:T(8,128)S(1)}, u32[]{:S(2)}) copy-start(f32[6,160]{1,0:T(8,128)S(1)} %fusion.38) | copy-start | bytes 11524
  222.2 35.3 %copy-start.6 = (f32[960,768]{1,0:T(8,128)}, f32[960,768]{1,0:T(8,128)S(1)}, u32[]{:S(2)}) copy-start(f32[960,768]{1,0:T(8,128)S(1)} %get-tuple-element.73) | copy-start | bytes 8847364
  222.2 1.5 copy-start.43
  222.2 1.5 copy-start.48
  257.5 17.2 %copy-start.7 = (f32[960,768]{1,0:T(8,128)S(1)}, f32[960,768]{1,0:T(8,128)}, u32[]{:S(2)}) copy-start(f32[960,768]{1,0:T(8,128)} %copy-done.6) | copy-start | bytes 8847364
  274.7 11.2 copy-start.49
  284.2 1.7 copy-start.10
  284.3 2.9 copy-start.9
  284.3 3.3 copy-start.16
  297.1 127.5 %reduce-scatter.9.cloned.1.call-start = ((), (), s32[]{:S(2)}) async-start(), calls=%async_computation.8 | async-start | bytes 11796480 | tf_op jit(solution)/shard_map/reduce_scatter | solution.py:185
  308.2 1.4 copy-start.17
  308.2 195.0 %reduce-scatter.11.cloned.1.call-start = ((), (), s32[]{:S(2)}) async-start(), calls=%async_computation.9 | async-start | bytes 11796480 | tf_op jit(solution)/shard_map/reduce_scatter | solution.py:186
  320.1 0.9 copy-start.20
  320.1 0.9 copy-start.22
  320.1 21.3 %copy-start.24 = (bf16[192,768]{1,0:T(8,128)(2,1)S(1)}, bf16[192,768]{1,0:T(8,128)(2,1)}, u32[]{:S(2)}) copy-start(bf16[192,768]{1,0:T(8,128)(2,1)} %param.17) | copy-start | bytes 884740
  320.2 423.8 %all-reduce.11.cloned.1.call-start = ((), (), s32[]{:S(2)}) async-start(), calls=%async_computation.10 | async-start | bytes 14155776 | tf_op jit(solution)/shard_map/psum | solution.py:194
  346.1 4.4 copy-start.28
  372.0 9.7 slice-start
  372.0 9.7 slice-start.1
  377.3 4.5 slice-start.2
  400.1 12.1 %copy-start.13 = (bf16[3840,192]{0,1:T(8,128)(2,1)S(1)}, bf16[3840,192]{0,1:T(8,128)(2,1)}, u32[]{:S(2)}) copy-start(bf16[3840,192]{0,1:T(8,128)(2,1)} %reshape.310) | copy-start | bytes 4423684
  412.1 5.0 copy-start.14
  503.2 336.5 %reduce-scatter.7.cloned.1.call-start = ((), (), s32[]{:S(2)}) async-start(), calls=%async_computation.7 | async-start | bytes 14745600 | tf_op jit(solution)/shard_map/reduce_scatter | solution.py:175
  513.2 0.7 copy-start.26
  513.2 1.9 copy-start.4
  515.1 2.2 copy-start.5
  517.3 2.2 copy-start.39
  517.3 3.2 copy-start.40
  517.3 3.2 copy-start.32
  517.3 3.3 copy-start.46
  517.3 3.3 copy-start.2
  520.6 319.1 %copy-start.38 = (f32[768]{0:T(1024)S(1)}, f32[768]{0:T(1024)}, u32[]{:S(2)}) copy-start(f32[768]{0:T(1024)} %param.20) | copy-start | bytes 9220
  747.0 96.9 %copy-start.36 = (f32[6,160]{1,0:T(8,128)S(1)}, f32[6,160]{1,0:T(8,128)}, u32[]{:S(2)}) copy-start(f32[6,160]{1,0:T(8,128)} %copy-done.35) | copy-start | bytes 11524
  844.0 15.0 %copy-start.30 = (f32[6,160]{1,0:T(8,128)S(1)}, f32[6,160]{1,0:T(8,128)}, u32[]{:S(2)}) copy-start(f32[6,160]{1,0:T(8,128)} %copy-done.29) | copy-start | bytes 11524
  844.0 15.0 %copy-start.34 = (f32[6,160]{1,0:T(8,128)S(1)}, f32[6,160]{1,0:T(8,128)}, u32[]{:S(2)}) copy-start(f32[6,160]{1,0:T(8,128)} %copy-done.33) | copy-start | bytes 11524
  844.0 15.0 %copy-start.42 = (f32[768]{0:T(1024)S(1)}, f32[768]{0:T(1024)}, u32[]{:S(2)}) copy-start(f32[768]{0:T(1024)} %param.24) | copy-start | bytes 9220
  1139.4 26.0 %copy-start.15 = (f32[768,768]{1,0:T(8,128)S(1)}, f32[768,768]{1,0:T(8,128)}, u32[]{:S(2)}) copy-start(f32[768,768]{1,0:T(8,128)} %get-tuple-element.105) | copy-start | bytes 7077892
  1161.7 2.9 copy-start.18
Sparse Core Ops, SparseCore 0:
  26.8 46.8 all-gather.2
  126.1 93.8 reduce-scatter.4
  297.2 44.1 all-gather.4
  343.8 78.4 reduce-scatter.8
  424.7 78.4 reduce-scatter.10
  508.1 235.8 all-reduce.10
  746.8 92.8 reduce-scatter.6
where the time goes:
time: 1190 us; the launch traced here: 1170 us
  waiting for transfers between devices  529 us (44%)
  other arithmetic  317 us (27%)
  matrix products  173 us (15%)
  local copies, waits for them, and re-layouts  97.6 us (8%)
  blocking collectives  39.1 us (3%)
  between operations  16.3 us (1%)
    scatter-add x3, other arithmetic, add_rows(): image_rows.at[positions].add(addend)  270 us
    psum x1, waiting for transfers between devices, shards(): lax.psum((qkv_part, out_part, up_part, down_part, gain_one_part, bias_one...  223 us
    reduce_scatter x1, waiting for transfers between devices, shards(): lax.psum_scatter(jnp.einsum('rc,dc->rd', grad_proj, w_qkv, preferred_elem...  92.7 us
    reduce_scatter x1, waiting for transfers between devices, shards(): lax.psum_scatter(grad_down, 'head', scatter_dimension=0, tiled=True)  78.6 us
    reduce_scatter x1, waiting for transfers between devices, shards(): lax.psum_scatter(jnp.dot(mixed_heads, w_out, preferred_element_type=jnp.f...  75.9 us
    all_gather x1, waiting for transfers between devices, shards(): lax.all_gather(normed_one, 'head', axis=0, tiled=True)  38.8 us
    dot_general x1, matrix products, shards(): pre_act = jnp.dot(normed_two, w_up, preferred_element_type=jnp.float32)  33.7 us
    gather x2, local copies, waits for them, and re-layouts, select_rows(): image_rows[positions]  31.8 us
  transfers between devices with their start and end apart: 7, of which 6 were waited for; matrix products, arithmetic and copies ran while one was open for 12% of the time, Pallas kernels for 0%

commit v1 on v0

--- a/solution.py
+++ b/solution.py
@@ -17,14 +17,22 @@
     return jax.nn.gelu(values, approximate=False)
 
 
-def select_rows(matrix, indices):
-    return jax.vmap(lambda image_rows, positions: image_rows[positions])(matrix, indices)
-
-
-def add_rows(matrix, indices, additions):
-    return jax.vmap(lambda image_rows, positions, addend: image_rows.at[positions].add(addend))(
-        matrix, indices, additions
-    )
+def slot_matrix(indices, length):
+    return (indices[:, :, None] == jnp.arange(length)[None, None, :]).astype(jnp.bfloat16)
+
+
+def select_rows(matrix, chosen):
+    return jnp.einsum("gcs,gsd->gcd", chosen, matrix, preferred_element_type=jnp.float32)
+
+
+def spread_rows(chosen, additions):
+    upper = lax.reduce_precision(additions, 8, 7)
+    lower = additions - upper
+    parts = [part.astype(jnp.bfloat16) for part in (upper, lower)]
+    spread = [
+        jnp.einsum("gcs,gcd->gsd", chosen, part, preferred_element_type=jnp.float32) for part in parts
+    ]
+    return spread[0] + spread[1]
 
 
 def masked_scores(query_rows, key_rows, key_valid):
@@ -119,23 +127,18 @@
     owned, length, features = tokens.shape
     capacity = slot_ids.shape[1]
     own_rows = owned * capacity
-    picked = select_rows(tokens, slot_ids).astype(jnp.float32)
+    chosen = slot_matrix(slot_ids, length)
+    picked = select_rows(tokens, chosen)
     own_valid = jnp.arange(capacity)[None, :] < counts[:, None]
     slot_mask = own_valid.astype(jnp.float32)
     normed_f, norm_pull = jax.vjp(layer_norm, picked, gain_one, bias_one)
     normed_one = normed_f.astype(jnp.bfloat16)
-    group_normed, group_counts = (
-        lax.all_gather(normed_one, "head", axis=0, tiled=True),
-        lax.all_gather(counts, "head", axis=0, tiled=True),
-    )
-    group_valid = jnp.arange(capacity)[None, :] < group_counts[:, None]
-    mixed_heads, kept_state = attend_forward(group_normed, group_valid, w_qkv)
-    attn_out = lax.psum_scatter(
-        jnp.dot(mixed_heads, w_out, preferred_element_type=jnp.float32),
-        "head",
-        scatter_dimension=0,
-        tiled=True,
-    ).reshape(owned, capacity, features)
+    w_qkv = lax.all_gather(w_qkv, "head", axis=1, tiled=True)
+    w_out = lax.all_gather(w_out, "head", axis=0, tiled=True)
+    mixed_heads, kept_state = attend_forward(normed_one, own_valid, w_qkv)
+    attn_out = jnp.dot(mixed_heads, w_out, preferred_element_type=jnp.float32).reshape(
+        owned, capacity, features
+    )
     hidden_in = picked + attn_out
     normed_two_f, norm_two_pull = jax.vjp(layer_norm, hidden_in, gain_two, bias_two)
     normed_two = normed_two_f.astype(jnp.bfloat16).reshape(own_rows, features)
@@ -148,10 +151,10 @@
     gate_value = jax.nn.sigmoid(jnp.sum(picked * w_router, axis=-1))
     weight_row = gate_value * slot_mask
     branch = attn_out + mlp_out
-    result = add_rows(tokens.astype(jnp.float32), slot_ids, weight_row[..., None] * branch).astype(
-        jnp.bfloat16
-    )
-    grad_picked_out = select_rows(cotangent, slot_ids).astype(jnp.float32)
+    result = (
+        tokens.astype(jnp.float32) + spread_rows(chosen, weight_row[..., None] * branch)
+    ).astype(jnp.bfloat16)
+    grad_picked_out = select_rows(cotangent, chosen)
     grad_branch = weight_row[..., None] * grad_picked_out
     grad_gate = slot_mask * jnp.sum(grad_picked_out * branch, axis=-1)
     grad_logits = grad_gate * gate_value * (1.0 - gate_value)
@@ -166,57 +169,47 @@
     ).reshape(owned, capacity, features)
     grad_hidden, grad_gain_two, grad_bias_two = norm_two_pull(grad_normed_two)
     grad_attn_b = (grad_branch + grad_hidden).astype(jnp.bfloat16).reshape(own_rows, features)
-    group_grad = lax.all_gather(grad_attn_b, "head", axis=0, tiled=True)
+    group_grad = grad_attn_b
     grad_mixed = jnp.einsum(
         "rd,ed->re", group_grad, w_out, preferred_element_type=jnp.float32
     ).astype(jnp.bfloat16)
     grad_wout = jnp.einsum("re,rd->ed", mixed_heads, group_grad, preferred_element_type=jnp.float32)
-    grad_proj, grad_wqkv_t = attend_backward(group_normed, group_valid, kept_state, grad_mixed)
-    grad_normed = lax.psum_scatter(
-        jnp.einsum("rc,dc->rd", grad_proj, w_qkv, preferred_element_type=jnp.float32),
-        "head",
-        scatter_dimension=0,
-        tiled=True,
+    grad_proj, grad_wqkv_t = attend_backward(normed_one, own_valid, kept_state, grad_mixed)
+    grad_normed = jnp.einsum(
+        "rc,dc->rd", grad_proj, w_qkv, preferred_element_type=jnp.float32
     ).reshape(owned, capacity, features)
     grad_picked, grad_gain_one, grad_bias_one = norm_pull(grad_normed)
     grad_rows = grad_picked + grad_hidden + grad_logits[..., None] * w_router
-    grad_tokens = add_rows(cotangent.astype(jnp.float32), slot_ids, grad_rows)
-    up_part, down_part, gain_one_part, bias_one_part, gain_two_part, bias_two_part, router_part = (
-        lax.psum_scatter(grad_up_t, "head", scatter_dimension=0, tiled=True),
-        lax.psum_scatter(grad_down, "head", scatter_dimension=0, tiled=True),
-        lax.psum_scatter(grad_gain_one, "head", scatter_dimension=0, tiled=True),
-        lax.psum_scatter(grad_bias_one, "head", scatter_dimension=0, tiled=True),
-        lax.psum_scatter(grad_gain_two, "head", scatter_dimension=0, tiled=True),
-        lax.psum_scatter(grad_bias_two, "head", scatter_dimension=0, tiled=True),
-        lax.psum_scatter(grad_router, "head", scatter_dimension=0, tiled=True),
-    )
-    qkv_part, out_part = (grad_wqkv_t, grad_wout)
-    summed = lax.psum(
-        (
-            qkv_part,
-            out_part,
-            up_part,
-            down_part,
-            gain_one_part,
-            bias_one_part,
-            gain_two_part,
-            bias_two_part,
-            router_part,
-        ),
-        "img",
+    grad_tokens = cotangent.astype(jnp.float32) + spread_rows(chosen, grad_rows)
+    parts = lax.axis_size("head")
+    me = lax.axis_index("head")
+
+    def reduced(matrix):
+        shard = lax.psum_scatter(
+            matrix.astype(jnp.bfloat16), "head", scatter_dimension=0, tiled=True
+        )
+        piece = lax.psum_scatter(shard, "img", scatter_dimension=0, tiled=True)
+        return lax.all_gather(piece, "img", axis=0, tiled=True).astype(jnp.float32)
+
+    vectors = lax.psum(
+        jnp.stack([grad_gain_one, grad_bias_one, grad_gain_two, grad_bias_two, grad_router]),
+        ("img", "head"),
+    )
+    vectors = lax.dynamic_slice_in_dim(
+        vectors, me * (features // parts), features // parts, axis=1
     )
     return (
         result,
         grad_tokens,
-        summed[0].T,
-        summed[1],
-        summed[2].T,
-        summed[3],
-        summed[4],
-        summed[5],
-        summed[6],
-        summed[7],
-        summed[8],
+        reduced(grad_wqkv_t).T,
+        reduced(grad_wout),
+        reduced(grad_up_t).T,
+        reduced(grad_down),
+        vectors[0],
+        vectors[1],
+        vectors[2],
+        vectors[3],
+        vectors[4],
     )
 
 

time: 1190 us -> 745 us (0.63)
  other arithmetic: 317 us -> 40.9 us
  waiting for transfers between devices: 529 us -> 270 us
  blocking collectives: 39.1 us -> 105 us
  local copies, waits for them, and re-layouts: 97.6 us -> 148 us
  matrix products: 173 us -> 158 us
    scatter-add x3 -> x0, other arithmetic: 270 us -> none  [add_rows(): image_rows.at[positions].add(addend)]
    psum x1 -> x0, waiting for transfers between devices: 223 us -> none  [shards(): lax.psum((qkv_part, out_part, up_part, down_part, gain_one_part, bias_one...]
    all_gather x0 -> x2, blocking collectives: none -> 64.3 us  [reduced(): return lax.all_gather(piece, 'img', axis=0, tiled=True).astype(jnp.float32)]
    reduce_scatter x4 -> x8, waiting for transfers between devices: 247 us -> 193 us  [the longest x4 155 us: reduced(): piece = lax.psum_scatter(shard, 'img', scatter_dimension=0, tiled=True)]
    unnamed x118 -> x148, local copies, waits for them, and re-layouts: 17.2 us -> 51.8 us
    gather x2 -> x0, local copies, waits for them, and re-layouts: 31.8 us -> none  [select_rows(): image_rows[positions]]
    dot_general x1, matrix products: 33.7 us -> 7.44 us  [shards(): pre_act = jnp.dot(normed_two, w_up, preferred_element_type=jnp.float32)]
    slice x1, local copies, waits for them, and re-layouts: 3.57 us -> 27.6 us  [attend_forward(): value_rows = projected[:, :, :, 2]]
  transfers between devices with their start and end apart: 7 -> 12, of which waited for: 6 -> 8; matrix products, arithmetic and copies ran while one was open for 12% -> 38% of each run, Pallas kernels for 0% -> 0%
where the time goes in v1:
time: 745 us; the launch traced here: 738 us
  waiting for transfers between devices  270 us (36%)
  matrix products  158 us (21%)
  local copies, waits for them, and re-layouts  148 us (20%)
  blocking collectives  105 us (14%)
  other arithmetic  40.9 us (5%)
  between operations  15.6 us (2%)
    reduce_scatter x4, waiting for transfers between devices, reduced(): piece = lax.psum_scatter(shard, 'img', scatter_dimension=0, tiled=True)  155 us
    all_gather x2, blocking collectives, reduced(): return lax.all_gather(piece, 'img', axis=0, tiled=True).astype(jnp.float32)  64.3 us
    unnamed x148, local copies, waits for them, and re-layouts  51.8 us
    all_gather x2, waiting for transfers between devices, reduced(): return lax.all_gather(piece, 'img', axis=0, tiled=True).astype(jnp.float32)  49.2 us
    psum x1, blocking collectives, shards(): lax.psum(jnp.stack([grad_gain_one, grad_bias_one, grad_gain_two, grad_bia...  40.3 us
    reduce_scatter x4, waiting for transfers between devices, reduced(): lax.psum_scatter(matrix.astype(jnp.bfloat16), 'head', scatter_dimension=0...  38.5 us
    dot_general x1, matrix products, shards(): jnp.einsum('rd,fd->rf', grad_mlp, w_down, preferred_element_type=jnp.floa...  32.1 us
    convert_element_type x3, local copies, waits for them, and re-layouts, attend_backward(): grad_proj = jnp.stack([grad_query, grad_key, grad_value], axis=3).astype(...  30.6 us
  transfers between devices with their start and end apart: 12, of which 8 were waited for; matrix products, arithmetic and copies ran while one was open for 38% of the time, Pallas kernels for 0%

profile of v1, /device:TPU:0, one launch (start us, length us, event | category | flops | bytes accessed | tf_op | source)
XLA Modules:
  0.0 738.2 jit_solution(14148129661258555415)
XLA Ops:
  9.5 2.4 fusion.69
  14.1 2.8 multiply_convert_fusion.2
  16.9 1.6 add_convert_fusion.4
  18.5 24.6 %all-gather.5.cloned.1.call-done = bf16[768,2304]{0,1:T(8,128)(2,1)} async-done(((bf16[768,576]{0,1:T(8,128)(2,1)}), bf16[768,2304]{0,1:T(8,128)(2,1)}) %all-gather.5.cloned.1.call-update) | async-done | bytes 3538960 | tf_op jit(solution)/shard_map/all_gather | solution.py:136
  43.1 8.1 %convolution_convert_fusion = bf16[960,2304]{1,0:T(8,128)(2,1)} fusion(bf16[960,768]{1,0:T(8,128)(2,1)} %bitcast.116, bf16[768,2304]{0,1:T(8,128)(2,1)} %all-gather.5.cloned.1.call-done), kind=kOutput, calls=%fused_computation.29 | convolution fusion | flops 3399598080 | bytes 9437184 | tf_op jit(solution)/shard_map/dot_general | solution.py:49
  51.2 19.0 %reshape.229 = bf16[6,160,12,3,64]{4,3,2,1,0:T(4,128)(2,1)} reshape(bf16[960,2304]{1,0:T(8,128)(2,1)} %convolution_convert_fusion) | data formatting | bytes 8847360 | tf_op jit(solution)/shard_map/reshape | solution.py:52
  70.2 27.6 %fusion.67 = (bf16[6,160,12,1,64]{4,3,2,1,0:T(2,128)(2,1)}, bf16[6,160,12,1,64]{4,3,2,1,0:T(2,128)(2,1)}, bf16[6,160,12,1,64]{4,3,2,1,0:T(2,128)(2,1)}) fusion(bf16[6,160,12,3,64]{4,3,2,1,0:T(4,128)(2,1)} %reshape.229), kind=kLoop, calls=%fused_computation.119 | loop fusion | bytes 8847360 | tf_op jit(solution)/shard_map/slice | solution.py:55
  97.8 12.1 %copy.63 = bf16[6,160,12,1,64]{1,4,2,0,3:T(8,128)(2,1)} copy(bf16[6,160,12,1,64]{4,3,2,1,0:T(2,128)(2,1)} %get-tuple-element.48) | data formatting | bytes 2949120
  109.8 12.1 %copy.64 = bf16[6,160,12,1,64]{1,4,2,0,3:T(8,128)(2,1)} copy(bf16[6,160,12,1,64]{4,3,2,1,0:T(2,128)(2,1)} %get-tuple-element.49) | data formatting | bytes 2949120
  121.9 12.1 %copy.65 = bf16[6,160,12,1,64]{1,4,2,0,3:T(8,128)(2,1)} copy(bf16[6,160,12,1,64]{4,3,2,1,0:T(2,128)(2,1)} %get-tuple-element.50) | data formatting | bytes 2949120
  134.0 5.6 fusion.12
  139.6 3.0 fusion.6
  142.7 1.7 copy-done
  145.0 4.5 fusion.34
  149.6 5.0 fusion.66
  156.4 7.4 %fusion.71 = f32[960,3072]{1,0:T(8,128)S(1)} fusion(bf16[960,768]{1,0:T(8,128)(2,1)S(1)} %bitcast.122, bf16[768,3072]{1,0:T(8,128)(2,1)} %param.18), kind=kOutput, calls=%fused_computation.123 | convolution fusion | flops 4529848320 | bytes 17989632 | tf_op jit(solution)/shard_map/dot_general | solution.py:145
  163.9 32.1 %add_convert_fusion = (bf16[960,3072]{1,0:T(8,128)(2,1)S(1)}, f32[960,3072]{1,0:T(8,128)}) fusion(f32[960,3072]{1,0:T(8,128)S(1)} %fusion.71, bf16[960,768]{1,0:T(8,128)(2,1)S(1)} %bitcast.118, bf16[3072,768]{1,0:T(8,128)(2,1)S(1)} %bitcast.131), kind=kOutput, calls=%fused_computation.5 | convolution fusion | flops 4742184960 | bytes 35684352 | tf_op jit(solution)/shard_map/rd,fd->rf/dot_general | solution.py:164
  195.9 2.5 copy-done.64
  198.4 6.9 convolution_convert_fusion.2
  205.4 10.1 %multiply_convert_fusion.1 = bf16[960,3072]{1,0:T(8,128)(2,1)S(1)} fusion(f32[960,3072]{1,0:T(8,128)} %get-tuple-element.45, f32[960,3072]{1,0:T(8,128)} %copy-done.14), kind=kLoop, calls=%fused_computation.7 | loop fusion | flops 8847360 | bytes 29491200 | tf_op jit(solution)/shard_map/convert_element_type | solution.py:147
  215.6 2.5 copy-done.22
  218.0 6.9 convolution_convert_fusion.1
  225.0 3.5 copy.50
  228.4 4.1 reshape.223
  232.5 8.5 %fusion.70 = (f32[768]{0:T(1024)S(1)}, f32[960,768]{1,0:T(8,128)S(1)}) fusion(bf16[960,3072]{1,0:T(8,128)(2,1)} %copy-done.64, bf16[768,3072]{1,0:T(8,128)(2,1)} %param.18), kind=kOutput, calls=%fused_computation.122 | convolution fusion | flops 4530584576 | bytes 13569024 | tf_op jit(solution)/shard_map/rf,df->rd/dot_general | solution.py:167
  241.1 1.1 multiply_reduce_fusion.1
  242.2 1.2 fusion.64
  244.1 7.5 %fusion.72 = f32[960,768]{1,0:T(8,128)S(1)} fusion(bf16[960,3072]{1,0:T(8,128)(2,1)S(1)} %bitcast.115, bf16[3072,768]{1,0:T(8,128)(2,1)} %param.19), kind=kOutput, calls=%fused_computation.124 | convolution fusion | flops 4529848320 | bytes 13565952 | tf_op jit(solution)/shard_map/dot_general | solution.py:148
  251.7 0.9 multiply_reduce_fusion.3
  253.8 1.3 convolution_convert_fusion.4
  255.2 4.2 reshape.230
  259.4 6.7 copy.42
  266.2 2.4 convolution_convert_fusion.5
  268.6 14.7 %multiply_reduce_fusion = (f32[6,12,160]{2,1,0:T(8,128)S(1)}, f32[6,12,160,160]{2,3,1,0:T(8,128)}) fusion(f32[6,12,160]{2,1,0:T(8,128)S(1)} %log_add_fusion, f32[6,12,160,160]{2,3,1,0:T(8,128)} %copy-done, pred[6,160]{1,0:T(8,128)(4,1)S(1)} %copy-done.52, bf16[6,160,12,64]{1,3,2,0:T(8,128)(2,1)} %copy.42, bf16[6,160,12,1,64]{1,4,2,0,3:T(8,128)(2,1)} %copy.63), kind=kOutput, calls=%fused_computation.4 | convolution fusion | flops 245134080 | bytes 17787840 | tf_op jit(solution)/shard_map/gqhe,gkhe->ghqk/dot_general | solution.py:83
  283.3 7.1 multiply_convert_fusion
  290.4 3.4 multiply_bitcast_fusion
  293.8 2.3 multiply_bitcast_fusion.1
  296.3 7.5 %fusion.31 = bf16[6,160,12,1,64]{1,4,2,0,3:T(8,128)(2,1)S(1)} fusion(bf16[6,160,12,64]{1,3,2,0:T(8,128)(2,1)S(1)} %copy-done.16, f32[6,12,160]{2,1,0:T(8,128)S(1)} %log_add_fusion, f32[6,12,160,160]{2,3,1,0:T(8,128)} %copy-done, pred[6,160]{1,0:T(8,128)(4,1)S(1)} %copy-done.52), kind=kOutput, calls=%fused_computation.72 | convolution fusion | flops 243302400 | bytes 10368960 | tf_op jit(solution)/shard_map/ghqk,gqhe->gkhe/dot_general | solution.py:77
  303.7 4.1 maximum_convert_fusion
  307.8 12.3 %copy.49 = bf16[6,160,12,3,64]{1,0,4,3,2:T(8,128)(2,1)} copy(bf16[6,160,12,3,64]{1,4,2,0,3:T(8,128)(2,1)} %maximum_convert_fusion) | data formatting | bytes 8847360 | tf_op jit(solution)/shard_map/convert_element_type | solution.py:100
  320.1 14.4 %convert_element_type.121 = bf16[960,2304]{0,1:T(8,128)(2,1)} reshape(bf16[6,160,12,3,64]{1,0,4,3,2:T(8,128)(2,1)} %copy.49) | data formatting | bytes 8847360 | tf_op jit(solution)/shard_map/convert_element_type | solution.py:100
  334.5 7.5 %convolution_convert_fusion.3 = bf16[2304,768]{1,0:T(8,128)(2,1)} fusion(bf16[960,2304]{0,1:T(8,128)(2,1)} %convert_element_type.121, bf16[960,768]{1,0:T(8,128)(2,1)S(1)} %bitcast.117), kind=kOutput, calls=%fused_computation.32 | convolution fusion | flops 3399155712 | bytes 9437184 | tf_op jit(solution)/shard_map/rc,rd->cd/dot_general | solution.py:103
  344.4 38.5 %reduce-scatter.9.cloned.1.call-done = bf16[576,768]{1,0:T(8,128)(2,1)} async-done(((bf16[2304,768]{1,0:T(8,128)(2,1)}), bf16[576,768]{1,0:T(8,128)(2,1)}) %reduce-scatter.9.cloned.1.call-update) | async-done | bytes 884752 | tf_op jit(solution)/shard_map/reduce_scatter | solution.py:188
  383.2 3.9 copy.47
  387.2 1.0 copy-done.63
  388.2 5.8 multiply_reduce_fusion.2
  394.0 56.4 %reduce-scatter.19.cloned.1.call-done = bf16[96,768]{1,0:T(8,128)(2,1)} async-done(((bf16[768,768]{1,0:T(8,128)(2,1)}), bf16[96,768]{1,0:T(8,128)(2,1)}) %reduce-scatter.19.cloned.1.call-update) | async-done | bytes 147472 | tf_op jit(solution)/shard_map/reduce_scatter | solution.py:191
  450.5 2.7 fusion.63
  454.1 1.4 fusion.39
  456.0 3.0 fusion.40
  459.0 2.6 add_convert_fusion.1
  461.6 55.2 %reduce-scatter.23.cloned.1.call-done = bf16[96,768]{1,0:T(8,128)(2,1)} async-done(((bf16[768,768]{1,0:T(8,128)(2,1)}), bf16[96,768]{1,0:T(8,128)(2,1)}) %reduce-scatter.23.cloned.1.call-update) | async-done | bytes 147472 | tf_op jit(solution)/shard_map/reduce_scatter | solution.py:191
  517.2 40.3 %psum.7 = f32[5,768]{1,0:T(8,128)S(1)} all-reduce(f32[5,768]{1,0:T(8,128)S(1)} %stack.39), channel_id=1, replica_groups=mesh['img'=8,'head'=4] {'img','head'}, use_global_device_ids=true, to_apply=%region_25.26 | all-reduce | flops 3840 | bytes 30720 | tf_op jit(solution)/shard_map/psum | solution.py:194
  558.2 7.8 %add_add_fusion.2 = f32[6,197,768]{2,1,0:T(8,128)} fusion(f32[6,197,768]{2,1,0:T(8,128)} %fusion.40, bf16[6,197,768]{2,1,0:T(8,128)(2,1)} %param.25, f32[6,160,768]{2,1,0:T(8,128)} %copy-done.11, f32[6,160,768]{2,1,0:T(8,128)} %copy-done.7, f32[6,160]{1,0:T(8,128)S(1)} %subtract_multiply_fusion, f32[6,160]{1,0:T(8,128)S(1)} %negate_multiply_fusion.1, ...), kind=kOutput, calls=%fused_computation.42 | convolution fusion | flops 299299008 | bytes 14994432 | tf_op jit(solution)/shard_map/gcs,gcd->gsd/dot_general | solution.py:33
  566.0 12.0 %reduce-scatter.15.cloned.1.call-done = bf16[24,768]{1,0:T(8,128)(2,1)} async-done(((bf16[192,768]{1,0:T(8,128)(2,1)}), bf16[24,768]{1,0:T(8,128)(2,1)}) %reduce-scatter.15.cloned.1.call-update) | async-done | bytes 36880 | tf_op jit(solution)/shard_map/reduce_scatter | solution.py:191
  578.0 31.3 %all_gather.21 = bf16[192,768]{1,0:T(8,128)(2,1)S(1)} all-gather(bf16[24,768]{1,0:T(8,128)(2,1)} %reduce-scatter.15.cloned.1.call-done), channel_id=1, replica_groups=mesh['img'=8,'head'=4] {'img'}, dimensions={0}, use_global_device_ids=true | all-gather | bytes 331776 | tf_op jit(solution)/shard_map/all_gather | solution.py:192
  610.1 31.1 %reduce-scatter.11.cloned.1.call-done = bf16[72,768]{1,0:T(8,128)(2,1)} async-done(((bf16[576,768]{1,0:T(8,128)(2,1)}), bf16[72,768]{1,0:T(8,128)(2,1)}) %reduce-scatter.11.cloned.1.call-update) | async-done | bytes 110608 | tf_op jit(solution)/shard_map/reduce_scatter | solution.py:191
  641.2 33.0 %all_gather.20 = bf16[576,768]{1,0:T(8,128)(2,1)S(1)} all-gather(bf16[72,768]{1,0:T(8,128)(2,1)} %reduce-scatter.11.cloned.1.call-done), channel_id=1, replica_groups=mesh['img'=8,'head'=4] {'img'}, dimensions={0}, use_global_device_ids=true | all-gather | bytes 995328 | tf_op jit(solution)/shard_map/all_gather | solution.py:192
  674.1 1.3 convert_bitcast_fusion.1
  675.5 10.4 %all-gather.9.cloned.1.call-done = bf16[768,768]{1,0:T(8,128)(2,1)} async-done(((bf16[96,768]{1,0:T(8,128)(2,1)}), bf16[768,768]{1,0:T(8,128)(2,1)}) %all-gather.9.cloned.1.call-update) | async-done | bytes 1179664 | tf_op jit(solution)/shard_map/all_gather | solution.py:192
  685.8 1.4 convert_bitcast_fusion
  687.3 2.0 copy.51
  689.2 38.8 %all-gather.11.cloned.1.call-done = bf16[768,768]{1,0:T(8,128)(2,1)} async-done(((bf16[96,768]{1,0:T(8,128)(2,1)}), bf16[768,768]{1,0:T(8,128)(2,1)}) %all-gather.11.cloned.1.call-update) | async-done | bytes 1179664 | tf_op jit(solution)/shard_map/all_gather | solution.py:192
  728.1 2.8 convert_element_type.127
  (194 shorter events, 14.9 us)
Async XLA Ops:
  7.2 4.7 copy-start.55
  7.2 35.9 %all-gather.5.cloned.1.call-start = ((), (), s32[]{:S(2)}) async-start(), calls=%async_computation.8 | async-start | bytes 4423680 | tf_op jit(solution)/shard_map/all_gather | solution.py:136
  7.9 141.6 %all-gather.7.cloned.1.call-start = ((), (), s32[]{:S(2)}) async-start(), calls=%async_computation.9 | async-start | bytes 1474560 | tf_op jit(solution)/shard_map/all_gather | solution.py:137
  8.7 333.5 %reduce-scatter.17.cloned.1.call-start = ((), (), s32[]{:S(2)}) async-start(), calls=%async_computation.14 | async-start | bytes 5898240 | tf_op jit(solution)/shard_map/reduce_scatter | solution.py:188
  9.4 133.2 %copy-start.51 = (pred[6,160]{1,0:T(8,128)(4,1)}, pred[6,160]{1,0:T(8,128)(4,1)S(1)}, u32[]{:S(2)}) copy-start(pred[6,160]{1,0:T(8,128)(4,1)S(1)} %iota_compare_fusion.7) | copy-start | bytes 2884
  9.4 3.9 copy-start.59
  9.5 4.6 copy-start.21
  9.5 4.6 copy-start.33
  11.8 137.7 %copy-start.1 = (f32[6,160,768]{2,1,0:T(8,128)}, f32[6,160,768]{2,1,0:T(8,128)S(1)}, u32[]{:S(2)}) copy-start(f32[6,160,768]{2,1,0:T(8,128)S(1)} %get-tuple-element.59) | copy-start | bytes 8847364
  11.8 5.0 copy-start.39
  14.0 2.8 copy-start.49
  14.0 2.8 copy-start.57
  14.0 2.8 copy-start.61
  139.6 4.8 copy-start
  139.6 4.8 copy-start.29
  139.6 5.4 copy-start.17
  155.7 8.1 %slice-start.5 = ((s8[4718592]{0:T(1024)(128)(4,1)}), s8[4194304]{0:T(1024)(128)(4,1)S(1)}, s32[]{:S(2)}) async-start(s8[4718592]{0:T(1024)(128)(4,1)} %bitcast.130), calls=%async_computation.25 | async-start | bytes 8388608
  156.3 7.5 %copy-start.26 = (bf16[6,160,768]{2,1,0:T(8,128)(2,1)}, bf16[6,160,768]{2,1,0:T(8,128)(2,1)S(1)}, u32[]{:S(2)}) copy-start(bf16[6,160,768]{2,1,0:T(8,128)(2,1)S(1)} %add_convert_fusion.3) | copy-start | bytes 4423684
  156.3 7.5 %copy-start.25 = (bf16[6,160,768]{2,1,0:T(8,128)(2,1)S(1)}, bf16[6,160,768]{2,1,0:T(8,128)(2,1)}, u32[]{:S(2)}) copy-start(bf16[6,160,768]{2,1,0:T(8,128)(2,1)} %get-tuple-element.62) | copy-start | bytes 4423684
  156.3 7.5 %slice-start.6 = ((s8[4718592]{0:T(1024)(128)(4,1)}), s8[524288]{0:T(1024)(128)(4,1)S(1)}, s32[]{:S(2)}) async-start(s8[4718592]{0:T(1024)(128)(4,1)} %bitcast.130), calls=%async_computation.26 | async-start | bytes 1048576
  163.8 32.1 %copy-start.14 = (f32[960,3072]{1,0:T(8,128)}, f32[960,3072]{1,0:T(8,128)S(1)}, u32[]{:S(2)}) copy-start(f32[960,3072]{1,0:T(8,128)S(1)} %fusion.71) | copy-start | bytes 35389444
  163.9 34.5 %copy-start.27 = (bf16[6,160,768]{2,1,0:T(8,128)(2,1)S(1)}, bf16[6,160,768]{2,1,0:T(8,128)(2,1)}, u32[]{:S(2)}) copy-start(bf16[6,160,768]{2,1,0:T(8,128)(2,1)} %copy-done.26) | copy-start | bytes 4423684
  195.9 2.5 copy-start.64
  205.4 137.5 %reduce-scatter.21.cloned.1.call-start = ((), (), s32[]{:S(2)}) async-start(), calls=%async_computation.17 | async-start | bytes 5898240 | tf_op jit(solution)/shard_map/reduce_scatter | solution.py:188
  215.5 2.5 copy-start.22
  224.9 118.7 %reduce-scatter.13.cloned.1.call-start = ((), (), s32[]{:S(2)}) async-start(), calls=%async_computation.12 | async-start | bytes 1474560 | tf_op jit(solution)/shard_map/reduce_scatter | solution.py:188
  232.5 8.5 %copy-start.4 = (f32[6,160,768]{2,1,0:T(8,128)S(1)}, f32[6,160,768]{2,1,0:T(8,128)}, u32[]{:S(2)}) copy-start(f32[6,160,768]{2,1,0:T(8,128)} %copy-done.3) | copy-start | bytes 8847364
  232.5 8.5 %copy-start.38 = (f32[6,160]{1,0:T(8,128)S(1)}, f32[6,160]{1,0:T(8,128)}, u32[]{:S(2)}) copy-start(f32[6,160]{1,0:T(8,128)} %copy-done.37) | copy-start | bytes 11524
  232.5 8.5 %copy-start.42 = (f32[6,160]{1,0:T(8,128)S(1)}, f32[6,160]{1,0:T(8,128)}, u32[]{:S(2)}) copy-start(f32[6,160]{1,0:T(8,128)} %copy-done.41) | copy-start | bytes 11524
  232.5 8.6 %copy-start.54 = (f32[768]{0:T(1024)S(1)}, f32[768]{0:T(1024)}, u32[]{:S(2)}) copy-start(f32[768]{0:T(1024)} %param.22) | copy-start | bytes 9220
  243.5 8.2 %copy-start.7 = (f32[6,160,768]{2,1,0:T(8,128)}, f32[6,160,768]{2,1,0:T(8,128)S(1)}, u32[]{:S(2)}) copy-start(f32[6,160,768]{2,1,0:T(8,128)S(1)} %get-tuple-element.43) | copy-start | bytes 8847364
  244.1 7.6 %copy-start.5 = (f32[6,160,768]{2,1,0:T(8,128)S(1)}, f32[6,160,768]{2,1,0:T(8,128)}, u32[]{:S(2)}) copy-start(f32[6,160,768]{2,1,0:T(8,128)} %get-tuple-element.64) | copy-start | bytes 8847364
  244.1 7.6 %copy-start.15 = (f32[6,160,768]{2,1,0:T(8,128)S(1)}, f32[6,160,768]{2,1,0:T(8,128)}, u32[]{:S(2)}) copy-start(f32[6,160,768]{2,1,0:T(8,128)} %get-tuple-element.63) | copy-start | bytes 8847364
  244.1 7.6 %copy-start.36 = (f32[6,160]{1,0:T(8,128)S(1)}, f32[6,160]{1,0:T(8,128)}, u32[]{:S(2)}) copy-start(f32[6,160]{1,0:T(8,128)} %copy-done.35) | copy-start | bytes 11524
  259.3 6.8 copy-start.30
  259.3 6.8 copy-start.32
  259.4 6.8 copy-start.23
  268.6 14.7 %slice-start = ((s8[11796480]{0:T(1024)(128)(4,1)}), s8[3407872]{0:T(1024)(128)(4,1)S(1)}, s32[]{:S(2)}) async-start(s8[11796480]{0:T(1024)(128)(4,1)} %bitcast.104), calls=%async_computation.20 | async-start | bytes 6815744
  268.6 14.7 %slice-start.1 = ((s8[11796480]{0:T(1024)(128)(4,1)}), s8[4194304]{0:T(1024)(128)(4,1)S(1)}, s32[]{:S(2)}) async-start(s8[11796480]{0:T(1024)(128)(4,1)} %bitcast.104), calls=%async_computation.21 | async-start | bytes 8388608
  268.6 14.7 %slice-start.2 = ((s8[11796480]{0:T(1024)(128)(4,1)}), s8[4194304]{0:T(1024)(128)(4,1)S(1)}, s32[]{:S(2)}) async-start(s8[11796480]{0:T(1024)(128)(4,1)} %bitcast.104), calls=%async_computation.22 | async-start | bytes 8388608
  283.3 7.1 copy-start.13
  290.4 3.4 copy-start.12
  296.2 86.7 %reduce-scatter.9.cloned.1.call-start = ((), (), s32[]{:S(2)}) async-start(), calls=%async_computation.10 | async-start | bytes 4423680 | tf_op jit(solution)/shard_map/reduce_scatter | solution.py:188
  296.2 7.5 %copy-start.18 = (bf16[6,160,12,1,64]{1,4,2,0,3:T(8,128)(2,1)S(1)}, bf16[6,160,12,1,64]{1,4,2,0,3:T(8,128)(2,1)}, u32[]{:S(2)}) copy-start(bf16[6,160,12,1,64]{1,4,2,0,3:T(8,128)(2,1)} %multiply_bitcast_fusion.1) | copy-start | bytes 4423684
  296.2 7.5 %copy-start.19 = (bf16[6,160,12,1,64]{1,4,2,0,3:T(8,128)(2,1)S(1)}, bf16[6,160,12,1,64]{1,4,2,0,3:T(8,128)(2,1)}, u32[]{:S(2)}) copy-start(bf16[6,160,12,1,64]{1,4,2,0,3:T(8,128)(2,1)} %multiply_bitcast_fusion) | copy-start | bytes 4423684
  320.1 14.4 %copy-start.24 = (bf16[6,160,768]{2,1,0:T(8,128)(2,1)S(1)}, bf16[6,160,768]{2,1,0:T(8,128)(2,1)}, u32[]{:S(2)}) copy-start(bf16[6,160,768]{2,1,0:T(8,128)(2,1)} %add_convert_fusion.4) | copy-start | bytes 4423684
  342.1 108.3 %reduce-scatter.19.cloned.1.call-start = ((), (), s32[]{:S(2)}) async-start(), calls=%async_computation.15 | async-start | bytes 1327104 | tf_op jit(solution)/shard_map/reduce_scatter | solution.py:191
  342.8 174.0 %reduce-scatter.23.cloned.1.call-start = ((), (), s32[]{:S(2)}) async-start(), calls=%async_computation.18 | async-start | bytes 1327104 | tf_op jit(solution)/shard_map/reduce_scatter | solution.py:191
  343.6 234.4 %reduce-scatter.15.cloned.1.call-start = ((), (), s32[]{:S(2)}) async-start(), calls=%async_computation.13 | async-start | bytes 331776 | tf_op jit(solution)/shard_map/reduce_scatter | solution.py:191
  344.3 296.9 %reduce-scatter.11.cloned.1.call-start = ((), (), s32[]{:S(2)}) async-start(), calls=%async_computation.11 | async-start | bytes 995328 | tf_op jit(solution)/shard_map/reduce_scatter | solution.py:191
  382.9 303.0 %all-gather.9.cloned.1.call-start = ((), (), s32[]{:S(2)}) async-start(), calls=%async_computation.16 | async-start | bytes 1327104 | tf_op jit(solution)/shard_map/all_gather | solution.py:192
  383.2 3.9 copy-start.2
  383.2 3.9 copy-start.40
  383.2 3.9 copy-start.50
  383.2 3.9 copy-start.58
  383.2 4.9 copy-start.63
  388.2 5.8 copy-start.46
  450.4 277.7 %all-gather.11.cloned.1.call-start = ((), (), s32[]{:S(2)}) async-start(), calls=%async_computation.19 | async-start | bytes 1327104 | tf_op jit(solution)/shard_map/all_gather | solution.py:192
  450.4 2.8 copy-start.44
  450.4 2.8 copy-start.60
  450.5 2.9 copy-start.6
  450.5 3.6 copy-start.10
  450.5 3.6 copy-start.34
  456.0 3.0 copy-start.20
  (20 other events, 29.8 us)
Sparse Core Ops, SparseCore 0:
  9.6 33.4 all-gather.4
  44.6 17.4 all-gather.6
  205.5 47.8 reduce-scatter.16
  255.9 47.8 reduce-scatter.20
  306.8 25.7 reduce-scatter.12
  342.2 40.6 reduce-scatter.8
  386.3 64.0 reduce-scatter.18
  453.7 63.0 reduce-scatter.22
  520.1 57.8 reduce-scatter.14
  581.2 59.9 reduce-scatter.10
  643.4 42.4 all-gather.8
  687.9 40.1 all-gather.10

commit v2 on v1

v2 whole, which is shorter than its diff:
```python
import functools

import jax
import jax.numpy as jnp
from jax import lax
from jax.experimental import pallas as pl
from jax.experimental.pallas import tpu as pltpu
from jax.sharding import PartitionSpec as P

HEAD_DIM = 64
EPS = 1e-06
BF = jnp.bfloat16
F32 = jnp.float32


def nn(a, b):
    return lax.dot_general(a, b, (((1,), (0,)), ((), ())), preferred_element_type=F32)


def nt(a, b):
    return lax.dot_general(a, b, (((1,), (1,)), ((), ())), preferred_element_type=F32)


def tn(a, b):
    return lax.dot_general(a, b, (((0,), (0,)), ((), ())), preferred_element_type=F32)


def standardise(values):
    average = jnp.mean(values, axis=-1, keepdims=True)
    centred = values - average
    variance = jnp.mean(centred * centred, axis=-1, keepdims=True)
    scale = lax.rsqrt(variance + EPS)
    return centred * scale, scale


def norm_pull(grad, unit, scale, gain):
    inner = grad * gain
    first = jnp.mean(inner, axis=-1, keepdims=True)
    second = jnp.mean(inner * unit, axis=-1, keepdims=True)
    return scale * (inner - first - unit * second)


def split_low(values):
    upper = values.astype(BF)
    return upper, (values - upper.astype(F32)).astype(BF)


def slot_table(slots, length):
    capacity = slots.shape[1]
    return (lax.broadcasted_iota(jnp.int32, (length, capacity), 0) == slots).astype(BF)


def row_gate(picked, w_router, count):
    gate = jax.nn.sigmoid(jnp.sum(picked * w_router, axis=-1, keepdims=True))
    valid = (lax.broadcasted_iota(jnp.int32, gate.shape, 0) < count).astype(F32)
    return gate, valid


def lane_low(shape):
    return lax.broadcasted_iota(jnp.int32, shape, 1) < HEAD_DIM


def head_scores(key_tile, query_tile, low, count):
    scores = nt(key_tile, query_tile)
    seen = lax.broadcasted_iota(jnp.int32, scores.shape, 0) < count
    return jnp.where(seen, scores, -1e30)


def swap_halves(tile):
    return pltpu.roll(tile.astype(F32), HEAD_DIM, 1).astype(BF)


def pair_tiles(proj, rows, pair):
    base = pair * 6 * HEAD_DIM
    tiles = [proj[rows, base + 2 * HEAD_DIM * t : base + 2 * HEAD_DIM * (t + 1)] for t in range(3)]
    low = lane_low(tiles[0].shape)
    zero = jnp.zeros_like(tiles[0])
    swapped = [swap_halves(tile) for tile in tiles]
    scale = HEAD_DIM ** (-0.5)
    query_a = jnp.where(low, tiles[0], zero) * jnp.asarray(scale, BF)
    query_b = jnp.where(low, swapped[1], zero) * jnp.asarray(scale, BF)
    return tiles, swapped, low, zero, ((swapped[0], query_a), (tiles[2], query_b))


def copy_in(source, target, sem):
    copy = pltpu.make_async_copy(source, target, sem)
    copy.start()
    return copy


def fused_kernel(
    owned, length, capacity, parts,
    slots, counts, gain_one, bias_one, gain_two, bias_two, w_router,
    tokens, cotangent, w_all, w_up, w_down,
    result_o, grad_tokens_o, down_o, up_o, qkv_out_o, vec_o, saved_o,
    wu, wd, ra, rs, down, up, normed_two, grad_mlp, mixed, attn, wide, picked, picked_grad,
    totals, logits, tok, cot, res, gtok,
    sems, tok_sems, cot_sems, res_sems, gtok_sems,
):
    features, hidden = w_up.shape
    columns = w_all.shape[0] - features
    pairs = columns // (6 * HEAD_DIM)
    proj = ra.at[:, 0:columns]
    normed_one = ra.at[:, columns : columns + features]
    width = features // 3

    def rows_of(i):
        return pl.ds(pl.multiple_of(i * capacity, 16), capacity)

    load_w = copy_in(w_all, down, sems.at[0])
    load_up = copy_in(w_up, wu, sems.at[1])
    load_down = copy_in(w_down, wd, sems.at[2])

    def token_copy(i, slot):
        return pltpu.make_async_copy(tokens.at[i], tok.at[slot], tok_sems.at[slot])

    def cot_copy(i, slot):
        return pltpu.make_async_copy(cotangent.at[i], cot.at[slot], cot_sems.at[slot])

    token_copy(0, 0).start()
    cot_copy(0, 0).start()

    @pl.loop(0, owned)
    def _(i):
        slot = lax.rem(i, 2)

        @pl.when(i + 1 < owned)
        def _():
            token_copy(i + 1, 1 - slot).start()
            cot_copy(i + 1, 1 - slot).start()

        rows = rows_of(i)
        table = slot_table(slots[i], length)
        token_copy(i, slot).wait()
        rows_f = tn(table, tok[slot])
        picked[rows, :] = rows_f.astype(BF)
        unit, _ = standardise(rows_f)
        normed_one[rows, :] = (unit * gain_one[...] + bias_one[...]).astype(BF)
        gate, valid = row_gate(rows_f, w_router[...], counts[i])
        cot_copy(i, slot).wait()
        grads = tn(table, cot[slot])
        picked_grad[rows, :] = grads.astype(BF)
        grad_mlp[rows, :] = (gate * valid * grads).astype(BF)

    load_w.wait()
    for n in range(3):
        cols = slice(n * features, (n + 1) * features)
        proj[:, cols] = nt(normed_one[...], down[cols, :]).astype(BF)
    save = copy_in(ra, saved_o, sems.at[3])

    @pl.loop(0, owned)
    def _(i):
        rows = rows_of(i)
        for pair in range(pairs):
            tiles, swapped, low, zero, heads = pair_tiles(proj, rows, pair)
            outs = []
            for h, (key_tile, query_tile) in enumerate(heads):
                scores = head_scores(key_tile, query_tile, low, counts[i])
                highest = jnp.max(scores, axis=0, keepdims=True)
                terms = jnp.exp(scores - highest)
                total = jnp.sum(terms, axis=0, keepdims=True)
                probs = (terms * (1.0 / total)).astype(BF)
                totals[i, 2 * pair + h : 2 * pair + h + 1, :] = highest + jnp.log(total)
                outs.append(tn(probs, tiles[1 + h]))
            mixed[rows, 2 * HEAD_DIM * pair : 2 * HEAD_DIM * (pair + 1)] = jnp.where(
                low, outs[0], outs[1]
            ).astype(BF)

    for n in range(3):
        cols = slice(n * width, (n + 1) * width)
        attn[:, cols] = nn(mixed[...], down[columns : columns + features, cols])

    @pl.loop(0, owned)
    def _(i):
        rows = rows_of(i)
        unit, _ = standardise(picked[rows, :].astype(F32) + attn[rows, :])
        normed_two[rows, :] = (unit * gain_two[...] + bias_two[...]).astype(BF)

    save.wait()
    load_up.wait()
    step = hidden // 6

    @pl.loop(0, 6)
    def _(n):
        cols = pl.ds(pl.multiple_of(n * step, 128), step)
        pre = nn(normed_two[...], wu[:, cols])
        below = 0.5 + 0.5 * lax.erf(pre * (0.5**0.5))
        ra[:, cols] = (pre * below).astype(BF)
        rs[:, cols] = (below + pre * (jnp.exp(-0.5 * pre * pre) * 0.3989422804014327)).astype(BF)

    @pl.loop(0, 6)
    def _(n):
        cols = pl.ds(pl.multiple_of(n * step, 128), step)
        down[cols, :] = tn(ra[:, cols], grad_mlp[...]).astype(BF)

    put_down = copy_in(down, down_o, sems.at[4])
    load_down.wait()

    @pl.loop(0, 6)
    def _(n):
        cols = pl.ds(pl.multiple_of(n * step, 128), step)
        rs[:, cols] = (nt(grad_mlp[...], wd[cols, :]) * rs[:, cols].astype(F32)).astype(BF)

    @pl.loop(0, parts)
    def _(h):
        cols = pl.ds(pl.multiple_of(h * (hidden // parts), 128), hidden // parts)
        up[:, cols] = tn(normed_two[...], rs[:, cols]).astype(BF)

    put_up = copy_in(up, up_o, sems.at[5])

    for n in range(3):
        cols = slice(n * width, (n + 1) * width)
        wide[:, cols] = nn(ra[...], wd[:, cols]) + attn[:, cols]

    reload = copy_in(saved_o, ra, sems.at[3])
    vec_o[...] = jnp.zeros_like(vec_o)

    def result_copy(i, slot):
        return pltpu.make_async_copy(res.at[slot], result_o.at[i], res_sems.at[slot])

    def gtok_copy(i, slot):
        return pltpu.make_async_copy(gtok.at[slot], grad_tokens_o.at[i], gtok_sems.at[slot])

    token_copy(0, 0).start()

    @pl.loop(0, owned)
    def _(i):
        slot = lax.rem(i, 2)

        @pl.when(i + 1 < owned)
        def _():
            token_copy(i + 1, 1 - slot).start()

        rows = rows_of(i)
        rows_f = picked[rows, :].astype(F32)
        gate, valid = row_gate(rows_f, w_router[...], counts[i])
        branch = wide[rows, :]
        logit = valid * gate * (1.0 - gate) * jnp.sum(
            picked_grad[rows, :].astype(F32) * branch, axis=-1, keepdims=True
        )
        logits[rows, :] = jnp.broadcast_to(logit, (capacity, 128))
        vec_o[4:5, :] += jnp.sum(logit * rows_f, axis=0, keepdims=True)
        table = slot_table(slots[i], length)
        upper, lower = split_low(gate * valid * branch)
        token_copy(i, slot).wait()

        @pl.when(i >= 2)
        def _():
            result_copy(i - 2, slot).wait()

        res[slot] = (tok[slot].astype(F32) + (nn(table, upper) + nn(table, lower))).astype(BF)
        result_copy(i, slot).start()

    for n in range(3):
        cols = slice(n * width, (n + 1) * width)
        wide[:, cols] = nt(rs[...], wu[cols, :])

    blocks = [copy_in(w_all.at[columns : columns + features], rs.at[0:features, 0:features], sems.at[6])]
    for n in range(3):
        blocks.append(
            copy_in(
                w_all.at[n * features : (n + 1) * features],
                rs.at[0:features, (n + 1) * features : (n + 2) * features],
                sems.at[7 + n],
            )
        )

    @pl.loop(0, owned)
    def _(i):
        rows = rows_of(i)
        rows_f = picked[rows, :].astype(F32)
        unit, scale = standardise(rows_f + attn[rows, :])
        grad = wide[rows, :]
        vec_o[2:3, :] += jnp.sum(grad * unit, axis=0, keepdims=True)
        vec_o[3:4, :] += jnp.sum(grad, axis=0, keepdims=True)
        back = norm_pull(grad, unit, scale, gain_two[...])
        wide[rows, :] = back
        gate, valid = row_gate(rows_f, w_router[...], counts[i])
        grad_mlp[rows, :] = (gate * valid * picked_grad[rows, :].astype(F32) + back).astype(BF)

    wd[columns : columns + features, :] = tn(mixed[...], grad_mlp[...]).astype(BF)
    blocks[0].wait()
    normed_two[...] = nt(grad_mlp[...], rs[0:features, 0:features]).astype(BF)
    reload.wait()

    @pl.loop(0, owned)
    def _(i):
        rows = rows_of(i)
        for pair in range(pairs):
            tiles, swapped, low, zero, heads = pair_tiles(proj, rows, pair)
            lanes = slice(2 * HEAD_DIM * pair, 2 * HEAD_DIM * (pair + 1))
            grads = normed_two[rows, lanes]
            halves = (jnp.where(low, grads, zero), jnp.where(low, zero, grads))
            found = []
            for h, (key_tile, query_tile) in enumerate(heads):
                scores = head_scores(key_tile, query_tile, low, counts[i])
                probs = jnp.exp(scores - totals[i, 2 * pair + h : 2 * pair + h + 1, :])
                grad_probs = nt(tiles[1 + h], halves[h])
                shift = jnp.sum(probs * grad_probs, axis=0, keepdims=True)
                grad_scores = (probs * (grad_probs - shift)).astype(BF)
                grad_value = nn(probs.astype(BF), grads)
                scale = HEAD_DIM ** (-0.5)
                if h == 0:
                    grad_query = tn(grad_scores, swapped[0]) * scale
                    grad_key = nn(grad_scores, swapped[0]) * scale
                else:
                    grad_query = tn(grad_scores, swapped[2]) * scale
                    grad_key = nn(grad_scores, swapped[1]) * scale
                found.append((grad_query, grad_key, grad_value))
            (query_a, key_a, value_a), (query_b, key_b, value_b) = found
            base = pair * 6 * HEAD_DIM
            proj[rows, base : base + 128] = jnp.where(low, query_a, key_a).astype(BF)
            proj[rows, base + 128 : base + 256] = jnp.where(low, value_a, query_b).astype(BF)
            proj[rows, base + 256 : base + 384] = jnp.where(low, key_b, value_b).astype(BF)

    for n in range(3):
        cols = slice(n * features, (n + 1) * features)
        wd[cols, :] = tn(proj[:, cols], normed_one[...]).astype(BF)
    put_qkv = copy_in(wd, qkv_out_o, sems.at[6])

    for n in range(3):
        blocks[1 + n].wait()
    for n in range(3):
        cols = slice(n * width, (n + 1) * width)
        total = nn(proj[:, 0:features], rs[0:features, features + n * width : features + (n + 1) * width])
        for k in range(1, 3):
            base = (k + 1) * features + n * width
            total += nn(proj[:, k * features : (k + 1) * features], rs[0:features, base : base + width])
        attn[:, cols] = total

    cot_copy(0, 0).start()

    @pl.loop(0, owned)
    def _(i):
        slot = lax.rem(i, 2)

        @pl.when(i + 1 < owned)
        def _():
            cot_copy(i + 1, 1 - slot).start()

        rows = rows_of(i)
        rows_f = picked[rows, :].astype(F32)
        unit, scale = standardise(rows_f)
        grad = attn[rows, :]
        vec_o[0:1, :] += jnp.sum(grad * unit, axis=0, keepdims=True)
        vec_o[1:2, :] += jnp.sum(grad, axis=0, keepdims=True)
        back = norm_pull(grad, unit, scale, gain_one[...])
        total = back + wide[rows, :] + logits[rows, 0:1] * w_router[...]
        table = slot_table(slots[i], length)
        upper, lower = split_low(total)
        cot_copy(i, slot).wait()

        @pl.when(i >= 2)
        def _():
            gtok_copy(i - 2, slot).wait()

        gtok[slot] = cot[slot].astype(F32) + (nn(table, upper) + nn(table, lower))
        gtok_copy(i, slot).start()

    for i in range(max(owned - 2, 0), owned):
        result_copy(i, i % 2).wait()
        gtok_copy(i, i % 2).wait()
    put_down.wait()
    put_up.wait()
    put_qkv.wait()


def fused(
    parts, tokens, slot_ids, counts, w_all, w_up, w_down,
    gain_one, bias_one, gain_two, bias_two, w_router, cotangent,
):
    owned, length, features = tokens.shape
    capacity = slot_ids.shape[1]
    rows = owned * capacity
    hidden = w_up.shape[1]
    columns = w_all.shape[0] - features
    heads = columns // (3 * HEAD_DIM)
    slots = slot_ids.reshape(owned, 1, capacity)
    vectors = [v.reshape(1, features) for v in (gain_one, bias_one, gain_two, bias_two, w_router)]
    S = jax.ShapeDtypeStruct
    inside = pl.BlockSpec(memory_space=pltpu.VMEM)
    outside = pl.BlockSpec(memory_space=pltpu.HBM)
    scalars = pl.BlockSpec(memory_space=pltpu.SMEM)
    V = pltpu.VMEM
    return pl.pallas_call(
        functools.partial(fused_kernel, owned, length, capacity, parts),
        out_shape=[
            S((owned, length, features), BF), S((owned, length, features), F32),
            S((hidden, features), BF), S((features, hidden), BF), S((columns + features, features), BF),
            S((8, features), F32), S((rows, columns + features), BF),
        ],
        in_specs=[inside, scalars] + [inside] * 5 + [outside] * 5,
        out_specs=[outside] * 5 + [inside, outside],
        scratch_shapes=[
            V((features, hidden), BF), V((hidden, features), BF), V((rows, hidden), BF),
            V((rows, hidden), BF), V((hidden, features), BF), V((features, hidden), BF),
            V((rows, features), BF), V((rows, features), BF), V((rows, features), BF),
            V((rows, features), F32), V((rows, features), F32), V((rows, features), BF),
            V((rows, features), BF), V((owned, heads, capacity), F32), V((rows, 128), F32),
            V((2, length, features), BF), V((2, length, features), BF), V((2, length, features), BF),
            V((2, length, features), F32),
            pltpu.SemaphoreType.DMA((10,)), pltpu.SemaphoreType.DMA((2,)), pltpu.SemaphoreType.DMA((2,)),
            pltpu.SemaphoreType.DMA((2,)), pltpu.SemaphoreType.DMA((2,)),
        ],
        compiler_params=pltpu.CompilerParams(vmem_limit_bytes=62 << 20),
    )(slots, counts, *vectors, tokens, cotangent, w_all, w_up, w_down)


def shards(
    tokens,
    slot_ids,
    counts,
    w_qkv,
    w_out,
    w_up,
    w_down,
    gain_one,
    bias_one,
    gain_two,
    bias_two,
    w_router,
    cotangent,
):
    features = tokens.shape[2]
    parts = lax.axis_size("head")
    me = lax.axis_index("head")
    w_all = jnp.concatenate(
        [
            lax.all_gather(w_qkv.T, "head", axis=0, tiled=True),
            lax.all_gather(w_out, "head", axis=0, tiled=True),
        ]
    )
    result, grad_tokens, down, up, both, vectors, _ = fused(
        parts, tokens, slot_ids, counts, w_all, w_up, w_down,
        gain_one, bias_one, gain_two, bias_two, w_router, cotangent,
    )
    columns = w_all.shape[0] - features

    def reduced(matrix, axis=0):
        shard = lax.psum_scatter(matrix, "head", scatter_dimension=axis, tiled=True)
        piece = lax.psum_scatter(shard, "img", scatter_dimension=0, tiled=True)
        return lax.all_gather(piece, "img", axis=0, tiled=True).astype(F32)

    vectors = lax.psum(vectors, ("img", "head"))
    vectors = lax.dynamic_slice_in_dim(
        vectors, me * (features // parts), features // parts, axis=1
    )
    return (
        result,
        grad_tokens,
        reduced(both[:columns]).T,
        reduced(both[columns:]),
        reduced(up, 1),
        reduced(down),
        vectors[0],
        vectors[1],
        vectors[2],
        vectors[3],
        vectors[4],
    )


def solution(mesh):
    return jax.shard_map(
        shards,
        mesh=mesh,
        in_specs=(
            P(("img", "head"), None, None),
            P(("img", "head"), None),
            P(("img", "head")),
            P(None, "head"),
            P("head", None),
            P(),
            P(),
            P(),
            P(),
            P(),
            P(),
            P(),
            P(("img", "head"), None, None),
        ),
        out_specs=(
            P(("img", "head"), None, None),
            P(("img", "head"), None, None),
            P(None, "head"),
            P("head", None),
            P(None, "head"),
            P("head", None),
            P("head"),
            P("head"),
            P("head"),
            P("head"),
            P("head"),
        ),
        check_vma=False,
    )
```

time: 745 us -> 707 us (0.949)
  waiting for transfers between devices: 270 us -> 445 us
  matrix products: 158 us -> 0 us
  local copies, waits for them, and re-layouts: 148 us -> 14.7 us
  Pallas kernels: 0 us -> 114 us
  other arithmetic: 40.9 us -> 12.6 us
    dot_general x25 -> x0, matrix products: 158 us -> none  [the longest x1 32.1 us: shards(): jnp.einsum('rd,fd->rf', grad_mlp, w_down, preferred_element_type=jnp.floa...]
    reduce_scatter x4, waiting for transfers between devices: 38.5 us -> 163 us  [reduced(): shard = lax.psum_scatter(matrix, 'head', scatter_dimension=axis, tiled=True)]
    pallas_call x0 -> x1, Pallas kernels: none -> 114 us  [fused(): pl.pallas_call(functools.partial(fused_kernel, owned, length, capacity, p...]
    unnamed x148 -> x2, local copies, waits for them, and re-layouts: 51.8 us -> 0.01 us
    convert_element_type x4 -> x0, local copies, waits for them, and re-layouts: 34 us -> none  [the longest x3 30.6 us: attend_backward(): grad_proj = jnp.stack([grad_query, grad_key, grad_value], axis=3).astype(...]
    reduce_scatter x4, waiting for transfers between devices: 155 us -> 185 us  [reduced(): piece = lax.psum_scatter(shard, 'img', scatter_dimension=0, tiled=True)]
    reshape x4 -> x6, local copies, waits for them, and re-layouts: 34 us -> 7.67 us  [the longest x5 6.38 us: fused(): v.reshape(1, features)]
    all_gather x4, waiting for transfers between devices: 73.8 us -> 95.5 us  [the longest x2 49.8 us: reduced(): return lax.all_gather(piece, 'img', axis=0, tiled=True).astype(F32)]
  transfers between devices with their start and end apart: 12 -> 12, of which waited for: 8 -> 12; matrix products, arithmetic and copies ran while one was open for 38% -> 3% of each run, Pallas kernels for 0% -> 0%
where the time goes in v2:
time: 707 us; the launch traced here: 706 us
  waiting for transfers between devices  445 us (63%)
  Pallas kernels  114 us (16%)
  blocking collectives  104 us (15%)
  local copies, waits for them, and re-layouts  14.7 us (2%)
  between operations  14.2 us (2%)
  other arithmetic  12.6 us (2%)
    reduce_scatter x4, waiting for transfers between devices, reduced(): piece = lax.psum_scatter(shard, 'img', scatter_dimension=0, tiled=True)  185 us
    reduce_scatter x4, waiting for transfers between devices, reduced(): shard = lax.psum_scatter(matrix, 'head', scatter_dimension=axis, tiled=True)  163 us
    pallas_call x1, Pallas kernels, fused(): pl.pallas_call(functools.partial(fused_kernel, owned, length, capacity, p...  114 us
    all_gather x2, blocking collectives, reduced(): return lax.all_gather(piece, 'img', axis=0, tiled=True).astype(F32)  64.3 us
    all_gather x2, waiting for transfers between devices, reduced(): return lax.all_gather(piece, 'img', axis=0, tiled=True).astype(F32)  49.8 us
    psum x1, blocking collectives, shards(): vectors = lax.psum(vectors, ('img', 'head'))  40.2 us
    all_gather x1, waiting for transfers between devices, shards(): lax.all_gather(w_qkv.T, 'head', axis=0, tiled=True)  32.4 us
  transfers between devices with their start and end apart: 12, of which 12 were waited for; matrix products, arithmetic and copies ran while one was open for 3% of the time, Pallas kernels for 0%

profile of v2, /device:TPU:0, one launch (start us, length us, event | category | flops | bytes accessed | tf_op | source)
XLA Modules:
  0.0 705.9 jit_solution(4354527631943118553)
XLA Ops:
  7.2 0.0 all-gather.7.cloned.1.call-start
  7.2 0.7 all-gather.7.cloned.1.call-update
  7.9 0.0 all-gather.5.cloned.1.call-start
  8.0 0.7 all-gather.5.cloned.1.call-update
  8.7 0.0 reduce-scatter.17.cloned.1.call-start
  8.7 1.3 reshape.40.slots
  10.0 1.3 reshape.41.gain_one
  11.3 1.3 reshape.42.bias_one
  12.5 1.3 reshape.43.gain_two
  13.8 1.3 reshape.44.bias_two
  15.1 1.3 reshape.45.w_router
  16.4 13.4 %all-gather.7.cloned.1.call-done = bf16[768,768]{1,0:T(8,128)(2,1)} async-done(((bf16[192,768]{1,0:T(8,128)(2,1)}), bf16[768,768]{1,0:T(8,128)(2,1)}) %all-gather.7.cloned.1.call-update) | async-done | bytes 1179664 | tf_op jit(solution)/shard_map/all_gather | solution.py:430
  29.8 32.4 %all-gather.5.cloned.1.call-done = bf16[2304,768]{1,0:T(8,128)(2,1)} async-done(((bf16[576,768]{1,0:T(8,128)(2,1)}), bf16[2304,768]{1,0:T(8,128)(2,1)}) %all-gather.5.cloned.1.call-update) | async-done | bytes 3538960 | tf_op jit(solution)/shard_map/all_gather | solution.py:429
  62.1 4.8 pad_maximum_fusion.w_all
  66.9 113.9 %shard_map.212 = (bf16[6,197,768]{2,1,0:T(8,128)(2,1)}, f32[6,197,768]{2,1,0:T(8,128)}, bf16[3072,768]{1,0:T(8,128)(2,1)}, bf16[768,3072]{1,0:T(8,128)(2,1)}, bf...) custom-call(s32[6,1,160]{2,1,0:T(1,128)} %reshape.40.slots, s32[6]{0:T(128)} %counts.1, ...), custom_call_target="tpu_custom_call" | custom-call | tf_op jit(solution)/shard_map/pallas_call | solution.py:385
  180.8 0.0 reduce-scatter.17.cloned.1.call-update
  180.8 0.0 reduce-scatter.21.cloned.1.call-start
  180.8 0.5 reduce-scatter.21.cloned.1.call-update
  181.4 0.0 reduce-scatter.13.cloned.1.call-start
  181.4 2.4 slice.22
  183.8 0.0 reduce-scatter.13.cloned.1.call-update
  183.8 0.0 reduce-scatter.9.cloned.1.call-start
  183.9 4.0 slice.21
  187.8 0.0 copy-start
  187.8 0.0 reduce-scatter.9.cloned.1.call-update
  187.9 0.0 reduce-scatter.19.cloned.1.call-start
  187.9 40.9 %reduce-scatter.17.cloned.1.call-done = bf16[768,768]{1,0:T(8,128)(2,1)} async-done(((bf16[768,3072]{1,0:T(8,128)(2,1)}), bf16[768,768]{1,0:T(8,128)(2,1)}) %reduce-scatter.17.cloned.1.call-update) | async-done | bytes 1179664 | tf_op jit(solution)/shard_map/reduce_scatter | solution.py:440
  228.8 0.0 reduce-scatter.19.cloned.1.call-update
  228.8 0.0 reduce-scatter.23.cloned.1.call-start
  228.8 50.4 %reduce-scatter.21.cloned.1.call-done = bf16[768,768]{1,0:T(8,128)(2,1)} async-done(((bf16[3072,768]{1,0:T(8,128)(2,1)}), bf16[768,768]{1,0:T(8,128)(2,1)}) %reduce-scatter.21.cloned.1.call-update) | async-done | bytes 1179664 | tf_op jit(solution)/shard_map/reduce_scatter | solution.py:440
  279.2 0.0 reduce-scatter.23.cloned.1.call-update
  279.2 0.0 reduce-scatter.15.cloned.1.call-start
  279.3 28.7 %reduce-scatter.13.cloned.1.call-done = bf16[192,768]{1,0:T(8,128)(2,1)} async-done(((bf16[768,768]{1,0:T(8,128)(2,1)}), bf16[192,768]{1,0:T(8,128)(2,1)}) %reduce-scatter.13.cloned.1.call-update) | async-done | bytes 294928 | tf_op jit(solution)/shard_map/reduce_scatter | solution.py:440
  308.0 0.0 reduce-scatter.15.cloned.1.call-update
  308.0 0.0 reduce-scatter.11.cloned.1.call-start
  308.0 43.0 %reduce-scatter.9.cloned.1.call-done = bf16[576,768]{1,0:T(8,128)(2,1)} async-done(((bf16[2304,768]{1,0:T(8,128)(2,1)}), bf16[576,768]{1,0:T(8,128)(2,1)}) %reduce-scatter.9.cloned.1.call-update) | async-done | bytes 884752 | tf_op jit(solution)/shard_map/reduce_scatter | solution.py:440
  351.0 0.0 reduce-scatter.11.cloned.1.call-update
  351.0 0.0 all-gather.9.cloned.1.call-start
  351.1 67.5 %reduce-scatter.19.cloned.1.call-done = bf16[96,768]{1,0:T(8,128)(2,1)} async-done(((bf16[768,768]{1,0:T(8,128)(2,1)}), bf16[96,768]{1,0:T(8,128)(2,1)}) %reduce-scatter.19.cloned.1.call-update) | async-done | bytes 147472 | tf_op jit(solution)/shard_map/reduce_scatter | solution.py:441
  418.6 0.0 all-gather.9.cloned.1.call-update
  418.6 0.0 all-gather.11.cloned.1.call-start
  418.7 66.4 %reduce-scatter.23.cloned.1.call-done = bf16[96,768]{1,0:T(8,128)(2,1)} async-done(((bf16[768,768]{1,0:T(8,128)(2,1)}), bf16[96,768]{1,0:T(8,128)(2,1)}) %reduce-scatter.23.cloned.1.call-update) | async-done | bytes 147472 | tf_op jit(solution)/shard_map/reduce_scatter | solution.py:441
  485.1 0.0 all-gather.11.cloned.1.call-update
  485.1 0.0 copy-done
  485.1 40.2 %psum.7 = f32[8,768]{1,0:T(8,128)S(1)} all-reduce(f32[8,768]{1,0:T(8,128)S(1)} %copy-done), channel_id=1, replica_groups=mesh['img'=8,'head'=4] {'img','head'}, use_global_device_ids=true, to_apply=%region_8.0 | all-reduce | flops 6144 | bytes 49152 | tf_op jit(solution)/shard_map/psum | solution.py:444
  525.3 0.7 fusion
  525.9 20.2 %reduce-scatter.15.cloned.1.call-done = bf16[24,768]{1,0:T(8,128)(2,1)} async-done(((bf16[192,768]{1,0:T(8,128)(2,1)}), bf16[24,768]{1,0:T(8,128)(2,1)}) %reduce-scatter.15.cloned.1.call-update) | async-done | bytes 36880 | tf_op jit(solution)/shard_map/reduce_scatter | solution.py:441
  546.1 31.5 %all_gather.21 = bf16[192,768]{1,0:T(8,128)(2,1)S(1)} all-gather(bf16[24,768]{1,0:T(8,128)(2,1)} %reduce-scatter.15.cloned.1.call-done), channel_id=1, replica_groups=mesh['img'=8,'head'=4] {'img'}, dimensions={0}, use_global_device_ids=true | all-gather | bytes 331776 | tf_op jit(solution)/shard_map/all_gather | solution.py:442
  577.7 0.9 convert_element_type.10
  578.5 30.9 %reduce-scatter.11.cloned.1.call-done = bf16[72,768]{1,0:T(8,128)(2,1)} async-done(((bf16[576,768]{1,0:T(8,128)(2,1)}), bf16[72,768]{1,0:T(8,128)(2,1)}) %reduce-scatter.11.cloned.1.call-update) | async-done | bytes 110608 | tf_op jit(solution)/shard_map/reduce_scatter | solution.py:441
  609.4 32.8 %all_gather.20 = bf16[576,768]{1,0:T(8,128)(2,1)S(1)} all-gather(bf16[72,768]{1,0:T(8,128)(2,1)} %reduce-scatter.11.cloned.1.call-done), channel_id=1, replica_groups=mesh['img'=8,'head'=4] {'img'}, dimensions={0}, use_global_device_ids=true | all-gather | bytes 995328 | tf_op jit(solution)/shard_map/all_gather | solution.py:442
  642.2 1.3 convert_bitcast_fusion
  643.5 10.6 %all-gather.9.cloned.1.call-done = bf16[768,768]{1,0:T(8,128)(2,1)} async-done(((bf16[96,768]{1,0:T(8,128)(2,1)}), bf16[768,768]{1,0:T(8,128)(2,1)}) %all-gather.9.cloned.1.call-update) | async-done | bytes 1179664 | tf_op jit(solution)/shard_map/all_gather | solution.py:442
  654.1 2.8 convert_element_type.11
  657.0 39.2 %all-gather.11.cloned.1.call-done = bf16[768,768]{1,0:T(8,128)(2,1)} async-done(((bf16[96,768]{1,0:T(8,128)(2,1)}), bf16[768,768]{1,0:T(8,128)(2,1)}) %all-gather.11.cloned.1.call-update) | async-done | bytes 1179664 | tf_op jit(solution)/shard_map/all_gather | solution.py:442
  696.2 2.8 convert_element_type.12
Async XLA Ops:
  7.2 22.6 %all-gather.7.cloned.1.call-start = ((), (), s32[]{:S(2)}) async-start(), calls=%async_computation.9 | async-start | bytes 1474560 | tf_op jit(solution)/shard_map/all_gather | solution.py:430
  7.9 54.2 %all-gather.5.cloned.1.call-start = ((), (), s32[]{:S(2)}) async-start(), calls=%async_computation.8 | async-start | bytes 4423680 | tf_op jit(solution)/shard_map/all_gather | solution.py:429
  8.7 220.1 %reduce-scatter.17.cloned.1.call-start = ((), (), s32[]{:S(2)}) async-start(), calls=%async_computation.14 | async-start | bytes 5898240 | tf_op jit(solution)/shard_map/reduce_scatter | solution.py:440
  180.8 98.4 %reduce-scatter.21.cloned.1.call-start = ((), (), s32[]{:S(2)}) async-start(), calls=%async_computation.17 | async-start | bytes 5898240 | tf_op jit(solution)/shard_map/reduce_scatter | solution.py:440
  181.4 126.6 %reduce-scatter.13.cloned.1.call-start = ((), (), s32[]{:S(2)}) async-start(), calls=%async_computation.12 | async-start | bytes 1474560 | tf_op jit(solution)/shard_map/reduce_scatter | solution.py:440
  183.8 167.2 %reduce-scatter.9.cloned.1.call-start = ((), (), s32[]{:S(2)}) async-start(), calls=%async_computation.10 | async-start | bytes 4423680 | tf_op jit(solution)/shard_map/reduce_scatter | solution.py:440
  187.8 297.2 %copy-start = (f32[8,768]{1,0:T(8,128)S(1)}, f32[8,768]{1,0:T(8,128)}, u32[]{:S(2)}) copy-start(f32[8,768]{1,0:T(8,128)} %get-tuple-element.22) | copy-start | bytes 73732
  187.9 230.7 %reduce-scatter.19.cloned.1.call-start = ((), (), s32[]{:S(2)}) async-start(), calls=%async_computation.15 | async-start | bytes 1327104 | tf_op jit(solution)/shard_map/reduce_scatter | solution.py:441
  228.8 256.3 %reduce-scatter.23.cloned.1.call-start = ((), (), s32[]{:S(2)}) async-start(), calls=%async_computation.18 | async-start | bytes 1327104 | tf_op jit(solution)/shard_map/reduce_scatter | solution.py:441
  279.2 266.9 %reduce-scatter.15.cloned.1.call-start = ((), (), s32[]{:S(2)}) async-start(), calls=%async_computation.13 | async-start | bytes 331776 | tf_op jit(solution)/shard_map/reduce_scatter | solution.py:441
  308.0 301.4 %reduce-scatter.11.cloned.1.call-start = ((), (), s32[]{:S(2)}) async-start(), calls=%async_computation.11 | async-start | bytes 995328 | tf_op jit(solution)/shard_map/reduce_scatter | solution.py:441
  351.0 303.1 %all-gather.9.cloned.1.call-start = ((), (), s32[]{:S(2)}) async-start(), calls=%async_computation.16 | async-start | bytes 1327104 | tf_op jit(solution)/shard_map/all_gather | solution.py:442
  418.6 277.6 %all-gather.11.cloned.1.call-start = ((), (), s32[]{:S(2)}) async-start(), calls=%async_computation.19 | async-start | bytes 1327104 | tf_op jit(solution)/shard_map/all_gather | solution.py:442
Sparse Core Ops, SparseCore 0:
  9.6 20.1 all-gather.6
  31.3 30.7 all-gather.4
  180.9 47.8 reduce-scatter.16
  231.3 47.8 reduce-scatter.20
  282.2 25.7 reduce-scatter.12
  310.6 40.4 reduce-scatter.8
  354.4 64.1 reduce-scatter.18
  422.0 63.0 reduce-scatter.22
  488.3 57.7 reduce-scatter.14
  549.4 59.9 reduce-scatter.10
  611.6 42.4 all-gather.8
  656.2 39.9 all-gather.10
